TPU v7x, 32 devices: a whole 2x2x4 slice. The times are simulated.
32 devices in a mesh: grp: 2 (over x), tile: 8 (over z, y), stn: 2 (over core).
Axes of the slice: x: 2, y: 2, z: 4, core: 2. Of those that a mesh axis runs over, the one named last changes fastest.
Arguments:
- samples: bfloat16 [512, 2, 126976], P(('grp', 'tile', 'stn')), parts along dimension 0, may hold values from -6 to 6
- filter_taps: float32 [16, 4096], replicated, may hold values from -1.5 to 1.5
- channel_list: int32 [768], P('grp'), parts along dimension 0, may hold values from 0 to 4095
- antenna_tile_lag: float32 [16, 512], P(None, ('grp', 'tile', 'stn')), parts along dimension 1, may hold values from -8 to 8
- tile_station_lag: float32 [16, 32], P(None, 'grp'), parts along dimension 1, may hold values from -64 to 64
- tile_of_antenna: int32 [512], P(('grp', 'tile', 'stn')), parts along dimension 0, may hold values from 0 to 15
- tile_station: int32 [32], P('grp'), parts along dimension 0, may hold values from 0 to 3, as said below
- tied_beam_pointing: int32 [2048], P('grp'), parts along dimension 0, may hold values from 0 to 15
- station_beam_lag: float32 [2048, 4], P('grp'), parts along dimension 0, may hold values from -256 to 256
Outputs:
- beam_power: float32 [2048, 384], P(('grp', 'tile', 'stn')), parts along dimension 0
There are 2 independent parts, one for each index of `grp`. A program takes and returns all parts, laid end to end along the dimension named above; an argument that names none is the same for every part. Nothing has to cross between parts.
Inputs may be any that keep to these rules, and one draw needn't show every extreme that they name: `tile_of_antenna`: tile numbers of the group. `tile_station`: station numbers of the group; every station holds at least one tile. `channel_list`: channel numbers below 4096, repeats allowed.
All inputs are finite; a program needn't handle non-finite values.
Results may differ from a plain program's by a relative error of at most 0.0019.
Values may be sent and summed in bfloat16 or wider, within the bound.
A program may use at most 192 MiB of HBM per device.

v0:
```python
import math

import jax
import jax.numpy as jnp
from jax import lax
from jax.sharding import PartitionSpec as P

OUTPUT_FRAMES = 16


TWO_PI = 6.283185307179586


def filter_bank(samples, filter_taps):
    num_taps, channels = filter_taps.shape
    frames = samples.shape[2] // channels - num_taps + 1
    blocks = samples.reshape(samples.shape[0], 2, frames + num_taps - 1, channels)
    filtered = blocks[:, :, 0:frames, :] * filter_taps[0]
    for tap_index in range(1, num_taps):
        filtered = (
            filtered + blocks[:, :, tap_index : tap_index + frames, :] * filter_taps[tap_index]
        )
    return filtered


def dft_table(channel_list, channels):
    sample_idx = lax.broadcasted_iota(jnp.int32, (channels, channel_list.shape[0]), 0)
    turn_count = sample_idx * channel_list[None, :] % channels
    angles = turn_count.astype(jnp.float32) * (TWO_PI / channels)
    factor = 1.0 / math.sqrt(channels)
    cosine = jnp.cos(angles) * factor
    sine_part = jnp.sin(angles) * factor
    upper_half = jnp.concatenate([cosine, -sine_part], axis=1)
    lower_half = jnp.concatenate([sine_part, cosine], axis=1)
    return jnp.stack([upper_half, lower_half])


def antenna_lags(antenna_tile_lag, tile_station_lag, tile_of_antenna, tile_station, stations):
    tile_count = tile_station_lag.shape[1]
    tile_ids = jnp.arange(tile_count, dtype=jnp.int32)
    matches = tile_of_antenna[:, None] == tile_ids[None, :]
    stn_extra = jnp.sum(jnp.where(matches[None, :, :], tile_station_lag[:, None, :], 0.0), axis=2)
    station = jnp.sum(jnp.where(matches, tile_station[None, :], 0), axis=1)
    tile_indicator = (station[None, :] == jnp.arange(stations, dtype=jnp.int32)[:, None]).astype(
        jnp.float32
    )
    return (antenna_tile_lag + stn_extra, tile_indicator)


def station_weight_matrix(antenna_lag, tile_indicator, frequency_radians):
    phase_angles = antenna_lag[:, :, None] * frequency_radians[None, None, :]
    cosine = jnp.cos(phase_angles)
    sine_part = jnp.sin(phase_angles)
    real_rows = jnp.stack([cosine, sine_part], axis=1)
    imag_rows = jnp.stack([-sine_part, cosine], axis=1)
    stacked_spectra = jnp.stack([real_rows, imag_rows], axis=1)
    weight_matrix = tile_indicator[:, None, None, None, :, None] * stacked_spectra[None]
    weight_matrix = weight_matrix.reshape(
        (tile_indicator.shape[0] * antenna_lag.shape[0],) + stacked_spectra.shape[1:]
    )
    return weight_matrix.astype(jnp.bfloat16)


def tied_beam_power(station_beam_output, pointing, beam_delay, frequency_radians, factor):
    chosen = jnp.take(station_beam_output, pointing, axis=3)
    angles = beam_delay.T[None, :, :] * frequency_radians[:, None, None]
    cosine = jnp.cos(angles)[..., None]
    sine_part = jnp.sin(angles)[..., None]
    real_part = jnp.sum(chosen[:, 0] * cosine + chosen[:, 1] * sine_part, axis=1)
    imag_part = jnp.sum(chosen[:, 1] * cosine - chosen[:, 0] * sine_part, axis=1)
    powers = jnp.sum(real_part * real_part + imag_part * imag_part, axis=2) * factor
    return powers.T


def body(
    samples,
    filter_taps,
    channel_list,
    antenna_tile_lag,
    tile_station_lag,
    tile_of_antenna,
    tile_station,
    tied_beam_pointing,
    station_beam_lag,
):
    devices = lax.axis_size(("tile", "stn"))
    own_rank = lax.axis_index(("tile", "stn"))
    channels = filter_taps.shape[1]
    stations = station_beam_lag.shape[1]
    pointings = tile_station_lag.shape[0]
    selected = channel_list.shape[0]
    antennas = samples.shape[0]
    dft_rows = dft_table(channel_list, channels).astype(jnp.bfloat16)
    filtered = filter_bank(samples, filter_taps).astype(jnp.bfloat16)
    channel_spectra = jnp.einsum(
        "arfn,rnk->afk", filtered, dft_rows, preferred_element_type=jnp.float32
    ).astype(jnp.bfloat16)
    spectra_split = channel_spectra.reshape(antennas, OUTPUT_FRAMES, 2, selected)
    antenna_lag, tile_indicator = antenna_lags(
        antenna_tile_lag, tile_station_lag, tile_of_antenna, tile_station, stations
    )
    frequency_radians = channel_list.astype(jnp.float32) * (TWO_PI / channels)
    factor = 1.0 / (OUTPUT_FRAMES * antennas * devices)
    term_width = 2 * stations * pointings * OUTPUT_FRAMES
    weight_matrix = station_weight_matrix(antenna_lag, tile_indicator, frequency_radians)
    partial_value = jnp.einsum(
        "qorac,afrc->coqf", weight_matrix, spectra_split, preferred_element_type=jnp.float32
    )
    reduced = lax.psum(partial_value.reshape(selected, term_width), ("tile", "stn"))
    station_beam_output = reduced.reshape(selected, 2, stations, pointings, OUTPUT_FRAMES)
    beam_share = tied_beam_pointing.shape[0] // devices
    own_points = lax.dynamic_slice_in_dim(tied_beam_pointing, own_rank * beam_share, beam_share)
    own_delay = lax.dynamic_slice_in_dim(station_beam_lag, own_rank * beam_share, beam_share)
    result = tied_beam_power(station_beam_output, own_points, own_delay, frequency_radians, factor)
    return result


def solution(mesh):
    in_specs = (
        P(("grp", "tile", "stn"), None, None),
        P(),
        P("grp"),
        P(None, ("grp", "tile", "stn")),
        P(None, "grp"),
        P(("grp", "tile", "stn")),
        P("grp"),
        P("grp"),
        P("grp", None),
    )
    out_specs = P(("grp", "tile", "stn"), None)
    return jax.shard_map(body, mesh=mesh, in_specs=in_specs, out_specs=out_specs, check_vma=False)
```

profile of v0, /device:TPU:0, one launch (start us, length us, event | category | flops | bytes accessed | tf_op | source)
XLA Modules:
  0.0 316.6 jit_solution(14323675898943925491)
XLA Ops:
  6.5 0.0 copy-start
  6.5 0.0 copy-start.5
  6.5 0.0 all-reduce.2.cloned.1.call-start
  6.5 28.5 %negate_convert_fusion = (bf16[4096,384]{1,0:T(8,128)(2,1)S(1)}, bf16[4096,384]{1,0:T(8,128)(2,1)}, bf16[4096,384]{1,0:T(8,128)(2,1)}) fusion(s32[384]{0:T(512)} %param.11), kind=kLoop, calls=%fused_computation.21 | loop fusion | flops 31457280 | bytes 9438720 | tf_op jit(solution)/shard_map/convert.7
  35.0 0.0 copy-done.5
  35.0 0.6 convert_multiply_fusion
  35.6 13.8 %reshape.114 = bf16[16,2,31,4096]{3,2,1,0:T(8,128)(2,1)} reshape(bf16[16,2,126976]{2,1,0:T(2,128)(2,1)} %param.9) | data formatting | bytes 16252928 | tf_op jit(solution)/shard_map/reshape | solution.py:17
  49.4 0.0 copy-start.3
  49.4 0.0 copy-start.1
  49.4 0.0 copy-start.2
  49.4 54.7 %fusion.16 = (bf16[16,2,16,4096]{3,2,1,0:T(8,128)(2,1)S(1)}, bf16[16,2,16,4096]{3,2,1,0:T(8,128)(2,1)}, bf16[16,2,16,4096]{3,2,1,0:T(8,128)(2,1)}, bf16[16,2,16,...) fusion(bf16[16,2,31,4096]{3,2,1,0:T(8,128)(2,1)} %reshape.114), kind=kLoop, calls=%fused_computation.52 | loop fusion | bytes 134217728 | tf_op jit(solution)/shard_map/slice | solution.py:18
  104.1 0.0 copy-done.3
  104.1 0.2 fusion.17
  104.3 0.0 copy-done.1
  104.3 0.0 copy-done.2
  104.3 4.8 %maximum_bitcast_fusion.2 = (bf16[1,4096,768]{2,1,0:T(8,128)(2,1)}, bf16[1,4096,768]{2,1,0:T(8,128)(2,1)}) fusion(bf16[4096,384]{1,0:T(8,128)(2,1)S(1)} %get-tuple-element.50, bf16[4096,384]{1,0:T(8,128)(2,1)S(1)} %copy-done.2, bf16[4096,384]{1,0:T(8,128)(2,1)S(1)} %copy-done.1), kind=kLoop, calls=%fused_computation.15 | loop fusion | flops 25165824 | bytes 22020096 | tf_op jit(solution)/shard_map/stack | solution.py:35
  109.2 27.6 %fusion.12 = bf16[16,16,768]{2,1,0:T(8,128)(2,1)S(1)} fusion(bf16[1,4096,768]{2,1,0:T(8,128)(2,1)} %get-tuple-element.26, bf16[1,4096,768]{2,1,0:T(8,128)(2,1)} %get-tuple-element.25, bf16[16,2,16,4096]{3,2,1,0:T(8,128)(2,1)} %get-tuple-element.24, bf16[16,2,16,4096]{3,2,1,0:T(8,128)(2,1)} %get-tuple-element.10, ...), kind=kOutput, calls=%fused_computation.32 | convolution fusion | flops 3328376832 | bytes 80347136 | tf_op jit(solution)/shard_map/arfn,rnk->afk/dot_general | solution.py:95
  136.8 0.1 reshape.97
  136.9 4.9 %copy.40 = bf16[16,16,2,384,1]{0,1,2,4,3:T(8,128)(2,1)S(1)} copy(bf16[16,16,2,384,1]{3,2,1,0,4:T(2,128)(2,1)S(1)} %bitcast.74) | data formatting | bytes 786432 | tf_op jit(solution)/shard_map/reshape | solution.py:98
  141.8 0.7 iota_compare_fusion
  142.5 0.9 select_reduce_fusion.1
  143.4 0.8 select_reduce_fusion
  144.2 0.7 add.97
  144.9 2.1 multiply_sine_fusion
  147.0 0.1 maximum_bitcast_fusion.8
  147.2 0.1 pad_maximum_fusion
  147.3 2.2 fusion.6
  149.5 12.3 %copy.34 = bf16[64,2,2,16,384]{0,3,2,1,4:T(8,128)(2,1)} copy(bf16[64,2,2,16,384]{4,3,2,1,0:T(8,128)(2,1)} %fusion.6) | data formatting | bytes 6291456 | tf_op jit(solution)/shard_map/convert_element_type | solution.py:61
  161.8 6.6 %convolution_bitcast_fusion = f32[384,2,64,16]{2,3,1,0:T(8,128)} fusion(bf16[16,16,2,384,1]{0,1,2,4,3:T(8,128)(2,1)S(1)} %copy.40, bf16[64,2,2,16,384]{0,3,2,1,4:T(8,128)(2,1)} %copy.34), kind=kOutput, calls=%fused_computation.28 | convolution fusion | flops 50331648 | bytes 6684672 | tf_op jit(solution)/shard_map/qorac,afrc->coqf/dot_general | solution.py:106
  168.4 6.0 %copy.35 = f32[384,2,64,16]{0,3,2,1:T(8,128)S(1)} copy(f32[384,2,64,16]{2,3,1,0:T(8,128)} %convolution_bitcast_fusion) | data formatting | bytes 6291456 | tf_op jit(solution)/shard_map/qorac,afrc->coqf/transpose | solution.py:106
  174.4 0.0 copy-start.4
  174.4 2.1 copy.36
  176.5 0.0 all-reduce.2.cloned.1.call-update
  176.5 0.0 copy-done
  176.6 0.1 dynamic-slice_bitcast_fusion
  176.6 0.1 copy.38
  176.7 0.8 compare_and_fusion
  177.5 0.0 copy-done.4
  177.5 3.1 multiply_cosine_fusion.1
  180.6 102.2 %all-reduce.2.cloned.1.call-done = f32[384,2,4,16,16]{0,4,1,2,3:T(8,128)} async-done(((f32[384,2,4,16,16]{0,4,1,2,3:T(8,128)}), f32[384,2,4,16,16]{0,4,1,2,3:T(8,128)}) %all-reduce.2.cloned.1.call-update) | async-done | bytes 3145744 | tf_op jit(solution)/shard_map/psum | solution.py:109
  282.8 7.8 %gather_fusion = f32[64,384,2,4,16]{1,4,2,3,0:T(8,128)} fusion(f32[384,2,4,16,16]{0,4,1,2,3:T(8,128)} %all-reduce.2.cloned.1.call-done, s32[1024]{0:T(1024)S(1)} %pad_clamp_fusion), kind=kCustom, calls=%fused_computation | custom fusion | bytes 25166080 | tf_op jit(solution)/shard_map/jit(_take)/gather | solution.py:65
  290.6 11.9 %select_bitcast_fusion = f32[384,2,4,64,16]{0,4,1,2,3:T(8,128)} fusion(f32[64,384,2,4,16]{1,4,2,3,0:T(8,128)} %gather_fusion, pred[64]{0:T(512)(128)(4,1)S(1)} %get-tuple-element.7), kind=kLoop, calls=%fused_computation.5 | loop fusion | flops 3145728 | bytes 25165888 | tf_op jit(solution)/shard_map/jit(_take)/select_n | solution.py:65
  302.5 6.2 %add_reduce_fusion = (f32[384,64,16]{0,2,1:T(8,128)S(1)}, f32[384,64,16]{0,2,1:T(8,128)S(1)}) fusion(f32[384,2,4,64,16]{0,4,1,2,3:T(8,128)} %select_bitcast_fusion, f32[384,4,64]{0,1,2:T(4,128)S(1)} %get-tuple-element.46, f32[384,4,64]{0,1,2:T(4,128)S(1)} %get-tuple-element.45), kind=kLoop, calls=%fused_computation.20 | loop fusion | flops 11796480 | bytes 16515072 | tf_op jit(solution)/shard_map/reduce_sum | solution.py:69
  308.7 0.4 add_reduce_fusion.1
  309.1 0.6 multiply_bitcast_fusion
  (3 shorter events, 0.0 us)
Async XLA Ops:
  6.5 170.0 %copy-start = (f32[1024,4]{0,1:T(4,128)S(1)}, f32[1024,4]{0,1:T(4,128)}, u32[]{:S(2)}) copy-start(f32[1024,4]{0,1:T(4,128)} %param.17) | copy-start | bytes 49156
  6.5 28.5 %copy-start.5 = (s32[384]{0:T(512)S(1)}, s32[384]{0:T(512)}, u32[]{:S(2)}) copy-start(s32[384]{0:T(512)} %param.11) | copy-start | bytes 4612
  6.5 276.3 %all-reduce.2.cloned.1.call-start = ((), (), s32[]{:S(2)}) async-start(), calls=%async_computation | async-start | bytes 6291456 | tf_op jit(solution)/shard_map/psum | solution.py:109
  49.4 54.7 %copy-start.3 = (f32[16,4096]{1,0:T(8,128)S(1)}, f32[16,4096]{1,0:T(8,128)}, u32[]{:S(2)}) copy-start(f32[16,4096]{1,0:T(8,128)} %param.10) | copy-start | bytes 786436
  49.4 54.9 %copy-start.1 = (bf16[4096,384]{1,0:T(8,128)(2,1)S(1)}, bf16[4096,384]{1,0:T(8,128)(2,1)}, u32[]{:S(2)}) copy-start(bf16[4096,384]{1,0:T(8,128)(2,1)} %get-tuple-element.51) | copy-start | bytes 9437188
  49.4 54.9 %copy-start.2 = (bf16[4096,384]{1,0:T(8,128)(2,1)S(1)}, bf16[4096,384]{1,0:T(8,128)(2,1)}, u32[]{:S(2)}) copy-start(bf16[4096,384]{1,0:T(8,128)(2,1)} %get-tuple-element.52) | copy-start | bytes 9437188
  174.4 3.1 copy-start.4
Sparse Core Ops, SparseCore 0:
  176.7 106.1 all-reduce.1
where the time goes:
time: 317 us
  local copies, waits for them, and re-layouts  102 us (32%)
  waiting for transfers between devices  102 us (32%)
  other arithmetic  64.6 us (20%)
  matrix products  34.2 us (11%)
  between operations  13.6 us (4%)
    psum x1, waiting for transfers between devices, body(): lax.psum(partial_value.reshape(selected, term_width), ('tile', 'stn'))  102 us
    slice x2, local copies, waits for them, and re-layouts, filter_bank(): filtered = blocks[:, :, 0:frames, :] * filter_taps[0]  54.9 us
    another operation x1, other arithmetic  28.5 us
    dot_general x1, matrix products, body(): jnp.einsum('arfn,rnk->afk', filtered, dft_rows, preferred_element_type=jn...  27.6 us
    reshape x1, local copies, waits for them, and re-layouts, filter_bank(): samples.reshape(samples.shape[0], 2, frames + num_taps - 1, channels)  13.8 us
    convert_element_type x1, local copies, waits for them, and re-layouts, station_weight_matrix(): return weight_matrix.astype(jnp.bfloat16)  12.3 us
    select_n x1, other arithmetic, tied_beam_power(): chosen = jnp.take(station_beam_output, pointing, axis=3)  11.9 us
    gather x1, local copies, waits for them, and re-layouts, tied_beam_power(): chosen = jnp.take(station_beam_output, pointing, axis=3)  7.81 us
  transfers between devices with their start and end apart: 1, of which 1 were waited for; matrix products, arithmetic and copies ran while one was open for 1% of the time, Pallas kernels for 0%

commit v1 on v0

v1 whole, which is shorter than its diff:
```python
import functools
import itertools
import math

import jax
import jax.numpy as jnp
from jax import lax
from jax.experimental import pallas as pl
from jax.experimental.pallas import tpu as pltpu
from jax.sharding import PartitionSpec as P

TWO_PI = 6.283185307179586
LANES = 128
CHUNK = 512
GROUP_AXES = ("tile", "stn")


def filter_dft_kernel(frames, taps, x_ref, taps_ref, ca_ref, sa_ref, cb_ref, sb_ref, out_ref, filt, table, acc):
    step = pl.program_id(0)
    antennas = x_ref.shape[2]
    selected = cb_ref.shape[0]
    rows = frames * antennas

    for piece in range(CHUNK // LANES):
        lanes = slice(piece * LANES, (piece + 1) * LANES)
        ca = ca_ref[0, :, piece : piece + 1]
        sa = sa_ref[0, :, piece : piece + 1]
        cb = cb_ref[...]
        sb = sb_ref[...]
        table[0:selected, lanes] = (ca * cb - sa * sb).astype(jnp.bfloat16)
        table[selected : 2 * selected, lanes] = (sa * cb + ca * sb).astype(jnp.bfloat16)
        weights = [
            jnp.broadcast_to(taps_ref[j : j + 1, lanes], (antennas, LANES)) for j in range(taps)
        ]
        for r in range(2):
            blocks = [
                x_ref[k, r, :, lanes].astype(jnp.float32) for k in range(frames + taps - 1)
            ]
            for f in range(frames):
                total = blocks[f] * weights[0]
                for j in range(1, taps):
                    total = total + blocks[f + j] * weights[j]
                start = r * rows + f * antennas
                filt[start : start + antennas, lanes] = total.astype(jnp.bfloat16)

    product = lax.dot_general(
        table[...], filt[...], (((1,), (1,)), ((), ())), preferred_element_type=jnp.float32
    )

    @pl.when(step == 0)
    def _():
        acc[...] = product

    @pl.when(step > 0)
    def _():
        acc[...] += product

    @pl.when(step == pl.num_programs(0) - 1)
    def _():
        out_ref[:, 0:rows] = (
            acc[0:selected, 0:rows] + acc[selected : 2 * selected, rows : 2 * rows]
        ).astype(jnp.bfloat16)
        out_ref[:, rows : 2 * rows] = (
            acc[0:selected, rows : 2 * rows] - acc[selected : 2 * selected, 0:rows]
        ).astype(jnp.bfloat16)


def unit_tables(sample_idx, channel_list, channels, factor):
    turn_count = sample_idx * channel_list[:, None] % channels
    angles = turn_count.astype(jnp.float32) * (TWO_PI / channels)
    return jnp.cos(angles) * factor, jnp.sin(angles) * factor


def channel_spectra(samples, filter_taps, channel_list):
    taps, channels = filter_taps.shape
    antennas = samples.shape[0]
    selected = channel_list.shape[0]
    blocks = samples.shape[2] // channels
    frames = blocks - taps + 1
    steps = channels // CHUNK
    pieces = CHUNK // LANES
    x = samples.reshape(antennas, 2, blocks, channels).transpose(2, 1, 0, 3)
    coarse = lax.broadcasted_iota(jnp.int32, (selected, channels // LANES), 1) * LANES
    fine = lax.broadcasted_iota(jnp.int32, (selected, LANES), 1)
    ca, sa = unit_tables(coarse, channel_list, channels, 1.0 / math.sqrt(channels))
    cb, sb = unit_tables(fine, channel_list, channels, 1.0)
    ca = ca.reshape(selected, steps, pieces).transpose(1, 0, 2)
    sa = sa.reshape(selected, steps, pieces).transpose(1, 0, 2)
    width = 2 * frames * antennas
    return pl.pallas_call(
        functools.partial(filter_dft_kernel, frames, taps),
        grid=(steps,),
        in_specs=[
            pl.BlockSpec((blocks, 2, antennas, CHUNK), lambda i: (0, 0, 0, i)),
            pl.BlockSpec((taps, CHUNK), lambda i: (0, i)),
            pl.BlockSpec((1, selected, pieces), lambda i: (i, 0, 0)),
            pl.BlockSpec((1, selected, pieces), lambda i: (i, 0, 0)),
            pl.BlockSpec((selected, LANES), lambda i: (0, 0)),
            pl.BlockSpec((selected, LANES), lambda i: (0, 0)),
        ],
        out_specs=pl.BlockSpec((selected, width), lambda i: (0, 0)),
        out_shape=jax.ShapeDtypeStruct((selected, width), jnp.bfloat16),
        scratch_shapes=[
            pltpu.VMEM((width, CHUNK), jnp.bfloat16),
            pltpu.VMEM((2 * selected, CHUNK), jnp.bfloat16),
            pltpu.VMEM((2 * selected, width), jnp.float32),
        ],
        compiler_params=pltpu.CompilerParams(vmem_limit_bytes=32 * 1024 * 1024),
    )(x, filter_taps, ca, sa, cb, sb)


def antenna_info(antenna_tile_lag, tile_station_lag, tile_of_antenna, tile_station):
    tile_ids = jnp.arange(tile_station_lag.shape[1], dtype=jnp.int32)
    matches = tile_of_antenna[:, None] == tile_ids[None, :]
    extra = jnp.sum(jnp.where(matches[None, :, :], tile_station_lag[:, None, :], 0.0), axis=2)
    station = jnp.sum(jnp.where(matches, tile_station[None, :], 0), axis=1)
    return jnp.concatenate([antenna_tile_lag + extra, station.astype(jnp.float32)[None]], axis=0)


def body(
    samples,
    filter_taps,
    channel_list,
    antenna_tile_lag,
    tile_station_lag,
    tile_of_antenna,
    tile_station,
    tied_beam_pointing,
    station_beam_lag,
):
    devices = lax.axis_size(GROUP_AXES)
    own_rank = lax.axis_index(GROUP_AXES)
    taps, channels = filter_taps.shape
    frames = samples.shape[2] // channels - taps + 1
    stations = station_beam_lag.shape[1]
    pointings = tile_station_lag.shape[0]
    selected = channel_list.shape[0]
    antennas = samples.shape[0]
    share = selected // devices
    beams = tied_beam_pointing.shape[0]

    info = antenna_info(antenna_tile_lag, tile_station_lag, tile_of_antenna, tile_station)
    info = lax.all_gather(info, GROUP_AXES, axis=1, tiled=True)
    lag = info[:pointings]
    mask = (
        info[pointings][None, :] == jnp.arange(stations, dtype=jnp.float32)[:, None]
    ).astype(jnp.bfloat16)

    own_channels = lax.dynamic_slice_in_dim(channel_list, own_rank * share, share)
    omega = own_channels.astype(jnp.float32) * (TWO_PI / channels)
    angles = lag[None] * omega[:, None, None]
    weights = jnp.concatenate([jnp.cos(angles), jnp.sin(angles)], axis=1).astype(jnp.bfloat16)
    theta = station_beam_lag.T[:, None, :] * omega[None, :, None]
    cosine = jnp.cos(theta)
    sine = jnp.sin(theta)
    onehot = (
        tied_beam_pointing[None, :] == jnp.arange(pointings, dtype=jnp.int32)[:, None]
    ).astype(jnp.float32)

    spectra = channel_spectra(samples, filter_taps, channel_list)
    spectra = lax.all_to_all(spectra, GROUP_AXES, split_axis=0, concat_axis=0, tiled=True)
    spectra = spectra.reshape(devices, share, 2 * frames, antennas).transpose(1, 2, 0, 3)
    spectra = spectra.reshape(share, 1, 2 * frames, devices * antennas)
    masked = (spectra * mask[None, :, None, :]).reshape(
        share, stations * 2 * frames, devices * antennas
    )
    terms = jnp.einsum("cua,cva->cuv", weights, masked, preferred_element_type=jnp.float32)
    terms = terms.reshape(share, 2, pointings, stations, 2, frames)
    real = terms[:, 0, :, :, 0] + terms[:, 1, :, :, 1]
    imag = terms[:, 0, :, :, 1] - terms[:, 1, :, :, 0]

    factor = 1.0 / (frames * antennas * devices)
    pairs = list(itertools.combinations(range(stations), 2))
    moments = [jnp.sum(real * real + imag * imag, axis=(2, 3)) * factor]
    for s, t in pairs:
        moments.append(
            jnp.sum(real[:, :, s] * real[:, :, t] + imag[:, :, s] * imag[:, :, t], axis=2)
            * (2.0 * factor)
        )
    for s, t in pairs:
        moments.append(
            jnp.sum(imag[:, :, s] * real[:, :, t] - real[:, :, s] * imag[:, :, t], axis=2)
            * (2.0 * factor)
        )
    moments = jnp.stack(moments).reshape(len(moments) * share, pointings)
    chosen = jnp.dot(moments, onehot, precision=lax.Precision.HIGHEST).reshape(-1, share, beams)
    power = chosen[0]
    for i, (s, t) in enumerate(pairs):
        power = power + chosen[1 + i] * (cosine[s] * cosine[t] + sine[s] * sine[t])
        power = power + chosen[1 + len(pairs) + i] * (sine[s] * cosine[t] - cosine[s] * sine[t])
    power = lax.all_to_all(power, GROUP_AXES, split_axis=1, concat_axis=0, tiled=True)
    return power.T


def solution(mesh):
    in_specs = (
        P(("grp", "tile", "stn"), None, None),
        P(),
        P("grp"),
        P(None, ("grp", "tile", "stn")),
        P(None, "grp"),
        P(("grp", "tile", "stn")),
        P("grp"),
        P("grp"),
        P("grp", None),
    )
    out_specs = P(("grp", "tile", "stn"), None)
    return jax.shard_map(body, mesh=mesh, in_specs=in_specs, out_specs=out_specs, check_vma=False)
```

time: 317 us -> 155 us (0.49)
  waiting for transfers between devices: 102 us -> 0.01 us
  local copies, waits for them, and re-layouts: 102 us -> 64.9 us
  other arithmetic: 64.6 us -> 30.1 us
  matrix products: 34.2 us -> 1.27 us
  blocking collectives: 0 us -> 32.1 us
  Pallas kernels: 0 us -> 18.2 us
  between operations: 13.6 us -> 0.59 us
  starting transfers between devices: 0.01 us -> 7.4 us
    psum x1 -> x0, waiting for transfers between devices: 102 us -> none  [body(): lax.psum(partial_value.reshape(selected, term_width), ('tile', 'stn'))]
    slice x2 -> x3, local copies, waits for them, and re-layouts: 54.9 us -> 1.11 us  [the longest x1 0.88 us: body(): power = power + chosen[1 + i] * (cosine[s] * cosine[t] + sine[s] * sine[t])]
    dot_general x2, matrix products: 34.2 us -> 1.27 us  [the longest x1 0.64 us: body(): jnp.dot(moments, onehot, precision=lax.Precision.HIGHEST)]
    another operation x4 -> x2, other arithmetic: 33.6 us -> 2.28 us
    all_gather x0 -> x1, blocking collectives: none -> 22.1 us  [body(): info = lax.all_gather(info, GROUP_AXES, axis=1, tiled=True)]
    pallas_call x0 -> x1, Pallas kernels: none -> 18.2 us  [channel_spectra(): pl.pallas_call(functools.partial(filter_dft_kernel, frames, taps), grid=(...]
    squeeze x0 -> x13, local copies, waits for them, and re-layouts: none -> 13.4 us  [the longest x6 6.45 us: body(): power = power + chosen[1 + i] * (cosine[s] * cosine[t] + sine[s] * sine[t])]
    select_n x1 -> x0, other arithmetic: 11.9 us -> none  [tied_beam_power(): chosen = jnp.take(station_beam_output, pointing, axis=3)]
  transfers between devices with their start and end apart: 1 -> 1, of which waited for: 1 -> 0; matrix products, arithmetic and copies ran while one was open for 1% -> 9% of each run, Pallas kernels for 0% -> 0%
where the time goes in v1:
time: 155 us
  local copies, waits for them, and re-layouts  64.9 us (42%)
  blocking collectives  32.1 us (21%)
  other arithmetic  30.1 us (19%)
  Pallas kernels  18.2 us (12%)
  starting transfers between devices  7.4 us (5%)
    reshape x2, local copies, waits for them, and re-layouts, channel_spectra(): x = samples.reshape(antennas, 2, blocks, channels).transpose(2, 1, 0, 3)  24.9 us
    all_gather x1, blocking collectives, body(): info = lax.all_gather(info, GROUP_AXES, axis=1, tiled=True)  22.1 us
    pallas_call x1, Pallas kernels, channel_spectra(): pl.pallas_call(functools.partial(filter_dft_kernel, frames, taps), grid=(...  18.2 us
    reduce_sum x2, other arithmetic, body(): jnp.sum(imag[:, :, s] * real[:, :, t] - real[:, :, s] * imag[:, :, t], ax...  13.3 us
    all_to_all x1, blocking collectives, body(): lax.all_to_all(power, GROUP_AXES, split_axis=1, concat_axis=0, tiled=True)  9.99 us
    all_to_all x1, starting transfers between devices, body(): lax.all_to_all(spectra, GROUP_AXES, split_axis=0, concat_axis=0, tiled=True)  7.4 us
    squeeze x6, local copies, waits for them, and re-layouts, body(): power = power + chosen[1 + i] * (cosine[s] * cosine[t] + sine[s] * sine[t])  6.45 us
    mul x1, other arithmetic, unit_tables(): return (jnp.cos(angles) * factor, jnp.sin(angles) * factor)  5.63 us
  transfers between devices with their start and end apart: 1, of which 0 were waited for; matrix products, arithmetic and copies ran while one was open for 9% of the time, Pallas kernels for 0%

profile of v1, /device:TPU:0, one launch (start us, length us, event | category | flops | bytes accessed | tf_op | source)
XLA Modules:
  0.0 154.6 jit_solution(14238335857596687243)
XLA Ops:
  0.0 13.8 %reshape.342 = bf16[16,2,31,4096]{3,2,1,0:T(8,128)(2,1)} reshape(bf16[16,2,126976]{2,1,0:T(2,128)(2,1)} %param.9) | data formatting | bytes 16252928 | tf_op jit(solution)/shard_map/reshape | solution.py:82
  13.8 11.1 %copy.90 = bf16[16,2,31,4096]{3,0,1,2:T(8,128)(2,1)} copy(bf16[16,2,31,4096]{3,2,1,0:T(8,128)(2,1)} %reshape.342) | data formatting | bytes 16252928 | tf_op jit(solution)/shard_map/reshape | solution.py:82
  24.9 0.8 fusion.12
  25.8 0.1 fusion.15
  25.9 0.5 copy.77
  26.4 5.6 %sine_multiply_fusion = (f32[8,384,4]{2,1,0:T(8,128)S(1)}, f32[8,384,4]{2,1,0:T(8,128)S(1)}) fusion(f32[8,384,4]{2,1,0:T(8,128)S(1)} %copy.77), kind=kLoop, calls=%fused_computation.2 | loop fusion | flops 36864 | bytes 147456 | tf_op jit(solution)/shard_map/mul | solution.py:71
  32.0 3.3 %copy-done = bf16[16,2,31,4096]{3,0,1,2:T(8,128)(2,1)S(1)} copy-done((bf16[16,2,31,4096]{3,0,1,2:T(8,128)(2,1)S(1)}, bf16[16,2,31,4096]{3,0,1,2:T(8,128)(2,1)}, u32[]{:S(2)}) %copy-start) | copy-done | bytes 8126488
  35.3 18.2 %shard_map.91 = bf16[384,512]{1,0:T(8,128)(2,1)} custom-call(bf16[31,2,16,4096]{3,2,1,0:T(8,128)(2,1)S(1)} %bitcast.57, f32[16,4096]{1,0:T(8,128)S(1)} %copy-done.1, f32[8,384,4]{2,1,0:T(8,128)S(1)} %get-tuple-element.27.ca_ref, f32[8,384,4]{2,1,0:T(8,128)S(1)} %get-tuple-element.26.sa_ref, f32[384,128]{1,0:T(8,128)S(1)} %get-tuple-element.58.cb_ref, ...), custom_call_target="tpu_custom_call" | custom-call | tf_op jit(solution)/shard_map/pallas_call | solution.py:90
  53.6 7.4 %all-to-all-start = ((bf16[16,24,512]{2,1,0:T(8,128)(2,1)}), bf16[16,24,512]{2,1,0:T(8,128)(2,1)S(1)}, u32[]{:S(2)}, u32[]{:S(2)}) async-start(bf16[16,24,512]{2,1,0:T(8,128)(2,1)} %bitcast.2), calls=%async_computation | async-start | bytes 786432 | tf_op jit(solution)/shard_map/all_to_all | solution.py:161
  61.0 0.1 convert_multiply_fusion
  61.1 1.4 multiply_cosine_fusion
  62.7 0.1 iota_compare_fusion.2
  62.8 0.2 select_reduce_fusion.1
  63.0 0.1 select_reduce_fusion
  63.1 0.1 copy.73
  63.2 22.1 %all_gather.3 = f32[17,256]{0,1:T(8,128)S(1)} all-gather(f32[17,16]{0,1:T(8,128)S(1)} %copy.73), channel_id=1, replica_groups=mesh['grp'=2,'tile'=8,'stn'=2] {'tile','stn'}, dimensions={1}, use_global_device_ids=true | all-gather | bytes 18496 | tf_op jit(solution)/shard_map/all_gather | solution.py:143
  85.3 0.1 copy.74
  85.4 0.8 sub.91
  86.2 0.8 add.184
  86.9 0.8 sub.89
  87.7 0.8 add.180
  88.5 0.8 sub.87
  89.3 0.8 add.176
  90.0 0.8 sub.85
  90.8 0.8 add.172
  91.6 0.8 sub.83
  92.4 0.8 add.168
  93.1 0.8 sub.81
  93.9 0.8 add.164
  94.7 0.2 slice_reduce_fusion
  94.8 2.3 %fusion = (bf16[24,16,256]{2,1,0:T(8,128)(2,1)}, bf16[24,16,256]{2,1,0:T(8,128)(2,1)}) fusion(f32[24]{0:T(128)S(1)} %convert_multiply_fusion, f32[16,256]{1,0:T(8,128)S(1)} %copy.74), kind=kLoop, calls=%fused_computation.11 | loop fusion | flops 294912 | bytes 409696 | tf_op jit(solution)/shard_map/convert
  97.1 2.5 %reshape.339 = bf16[16,24,32,16]{3,2,1,0:T(8,128)(2,1)S(1)} reshape(bf16[16,24,512]{2,1,0:T(8,128)(2,1)S(1)} %all-to-all-done) | data formatting | bytes 786432 | tf_op jit(solution)/shard_map/reshape | solution.py:162
  99.6 2.4 %copy.78 = bf16[24,32,16,16]{1,3,2,0:T(8,128)(2,1)} copy(bf16[24,32,16,16]{3,1,0,2:T(8,128)(2,1)S(1)} %bitcast.58) | data formatting | bytes 786432 | tf_op jit(solution)/shard_map/transpose | solution.py:162
  102.1 1.7 %copy.79 = bf16[24,32,256]{2,1,0:T(8,128)(2,1)S(1)} copy(bf16[24,32,256]{1,2,0:T(8,128)(2,1)} %bitcast.62) | data formatting | bytes 786432 | tf_op jit(solution)/shard_map/mul | solution.py:164
  103.8 0.1 bitcast_multiply_fusion
  103.9 0.6 fusion.2
  104.6 4.1 %reshape.340 = f32[24,2,16,4,2,16]{5,4,3,2,1,0:T(2,128)S(1)} reshape(f32[24,32,128]{2,1,0:T(8,128)S(1)} %fusion.2) | data formatting | bytes 786432 | tf_op jit(solution)/shard_map/reshape | solution.py:168
  108.6 2.1 %fusion.20 = (f32[24,1,16,4,1,16]{5,4,3,2,1,0:T(1,128)S(1)}, f32[24,1,16,4,1,16]{5,4,3,2,1,0:T(1,128)S(1)}, f32[24,1,16,4,1,16]{5,4,3,2,1,0:T(1,128)S(1)}) fusion(f32[24,2,16,4,2,16]{5,4,3,2,1,0:T(2,128)S(1)} %reshape.340), kind=kLoop, calls=%fused_computation.87 | loop fusion | flops 24576 | bytes 688128 | tf_op jit(solution)/shard_map/slice | solution.py:169
  110.7 1.0 add_reduce_fusion
  111.8 5.0 %subtract_reduce_fusion.5 = (f32[24,16]{1,0:T(8,128)S(1)}, f32[24,16]{1,0:T(8,128)S(1)}, f32[24,16]{1,0:T(8,128)S(1)}, f32[24,16]{1,0:T(8,128)S(1)}) fusion(f32[24,16,4,16]{3,2,1,0:T(4,128)S(1)} %bitcast.60, f32[24,16,4,16]{3,2,1,0:T(4,128)S(1)} %get-tuple-element.18), kind=kLoop, calls=%fused_computation.29 | loop fusion | flops 96768 | bytes 202752 | tf_op jit(solution)/shard_map/reduce_sum | solution.py:182
  116.8 8.3 %subtract_reduce_fusion.1 = (f32[24,16]{1,0:T(8,128)S(1)}, f32[24,16]{1,0:T(8,128)S(1)}, f32[24,16]{1,0:T(8,128)S(1)}, f32[24,16]{1,0:T(8,128)S(1)}, f32[24,16]{...) fusion(f32[24,16,4,16]{3,2,1,0:T(4,128)S(1)} %bitcast.61, ...), kind=kLoop, calls=%fused_computation.25 | loop fusion | flops 193536 | bytes 208896 | tf_op jit(solution)/shard_map/reduce_sum | solution.py:182
  125.3 0.6 fusion.14
  125.9 0.9 fusion.21
  126.8 0.1 squeeze.38
  126.9 0.1 squeeze.37
  127.1 0.1 squeeze.36
  127.2 0.1 squeeze.35
  127.3 0.1 squeeze.34
  127.4 1.3 squeeze.33
  128.7 1.7 %squeeze.32 = f32[24,16,64]{2,1,0:T(8,128)} reshape(f32[24,1024]{1,0:T(8,128)} %get-tuple-element.35) | data formatting | bytes 196608 | tf_op jit(solution)/shard_map/squeeze | solution.py:190
  130.3 1.7 %squeeze.31 = f32[24,16,64]{2,1,0:T(8,128)} reshape(f32[24,1024]{1,0:T(8,128)} %get-tuple-element.36) | data formatting | bytes 196608 | tf_op jit(solution)/shard_map/squeeze | solution.py:189
  132.0 1.7 %squeeze.30 = f32[24,16,64]{2,1,0:T(8,128)} reshape(f32[24,1024]{1,0:T(8,128)} %get-tuple-element.37) | data formatting | bytes 196608 | tf_op jit(solution)/shard_map/squeeze | solution.py:190
  133.6 1.7 %squeeze.29 = f32[24,16,64]{2,1,0:T(8,128)} reshape(f32[24,1024]{1,0:T(8,128)} %get-tuple-element.38) | data formatting | bytes 196608 | tf_op jit(solution)/shard_map/squeeze | solution.py:189
  135.3 1.7 %squeeze.28 = f32[24,16,64]{2,1,0:T(8,128)} reshape(f32[24,1024]{1,0:T(8,128)} %get-tuple-element.39) | data formatting | bytes 196608 | tf_op jit(solution)/shard_map/squeeze | solution.py:190
  136.9 1.7 %squeeze.26 = f32[24,16,64]{2,1,0:T(8,128)} reshape(f32[24,1024]{1,0:T(8,128)} %get-tuple-element.40) | data formatting | bytes 196608 | tf_op jit(solution)/shard_map/squeeze | solution.py:187
  138.6 1.7 %squeeze.27 = f32[24,16,64]{2,1,0:T(8,128)} reshape(f32[24,1024]{1,0:T(8,128)} %get-tuple-element.28) | data formatting | bytes 196608 | tf_op jit(solution)/shard_map/squeeze | solution.py:189
  140.4 1.7 %multiply_add_fusion = f32[24,16,64]{2,1,0:T(8,128)S(1)} fusion(f32[24,16,64]{2,1,0:T(8,128)S(1)} %squeeze.38, f32[24,16,64]{2,1,0:T(8,128)S(1)} %copy-done.2, f32[24,16,64]{2,1,0:T(8,128)S(1)} %squeeze.37, f32[24,16,64]{2,1,0:T(8,128)S(1)} %copy-done.3, f32[24,16,64]{2,1,0:T(8,128)S(1)} %squeeze.36, f32[24,16,64]{2,1,0:T(8,128)S(1)} %copy-done.4, ...), kind=kLoop, calls=%fused_computation.23 | loop fusion | flops 589824 | bytes 2555904 | tf_op jit(solution)/shard_map/add | solution.py:190
  142.1 0.1 copy.91
  142.2 0.2 reshape.344
  142.3 10.0 %all_to_all.25 = f32[16,1,1536]{2,1,0:T(1,128)S(1)} all-to-all(f32[16,1,1536]{2,1,0:T(1,128)S(1)} %reshape.344), channel_id=1, replica_groups=mesh['grp'=2,'tile'=8,'stn'=2] {'tile','stn'}, dimensions={0} | all-to-all | bytes 196608 | tf_op jit(solution)/shard_map/all_to_all | solution.py:191
  152.3 0.5 broadcast.234
  152.8 0.9 reduce.14
  153.7 0.1 reshape.345
  153.8 0.8 copy.83
  (68 shorter events, 0.4 us)
Async XLA Ops:
  13.8 11.1 %copy-start.17 = (s32[384]{0:T(512)S(1)}, s32[384]{0:T(512)}, u32[]{:S(2)}) copy-start(s32[384]{0:T(512)} %param.11) | copy-start | bytes 4612
  26.4 5.7 %copy-start.1 = (f32[16,4096]{1,0:T(8,128)S(1)}, f32[16,4096]{1,0:T(8,128)}, u32[]{:S(2)}) copy-start(f32[16,4096]{1,0:T(8,128)} %taps_ref.1) | copy-start | bytes 786436
  32.0 3.3 %copy-start = (bf16[16,2,31,4096]{3,0,1,2:T(8,128)(2,1)S(1)}, bf16[16,2,31,4096]{3,0,1,2:T(8,128)(2,1)}, u32[]{:S(2)}) copy-start(bf16[16,2,31,4096]{3,0,1,2:T(8,128)(2,1)} %copy.90) | copy-start | bytes 24379396
  35.3 25.8 %copy-start.16 = (f32[1024,4]{0,1:T(4,128)S(1)}, f32[1024,4]{0,1:T(4,128)}, u32[]{:S(2)}) copy-start(f32[1024,4]{0,1:T(4,128)} %param.17) | copy-start | bytes 49156
  53.6 43.5 %all-to-all-start = ((bf16[16,24,512]{2,1,0:T(8,128)(2,1)}), bf16[16,24,512]{2,1,0:T(8,128)(2,1)S(1)}, u32[]{:S(2)}, u32[]{:S(2)}) async-start(bf16[16,24,512]{2,1,0:T(8,128)(2,1)} %bitcast.2), calls=%async_computation | async-start | bytes 786432 | tf_op jit(solution)/shard_map/all_to_all | solution.py:161
  61.0 1.7 %copy-start.21 = (s32[16]{0:T(128)S(1)}, s32[16]{0:T(128)}, u32[]{:S(2)}) copy-start(s32[16]{0:T(128)} %param.14) | copy-start | bytes 196
  61.0 1.8 %copy-start.22 = (s32[16]{0:T(128)S(1)}, s32[16]{0:T(128)}, u32[]{:S(2)}) copy-start(s32[16]{0:T(128)} %param.15) | copy-start | bytes 196
  61.0 1.9 %copy-start.19 = (f32[16,16]{1,0:T(8,128)S(1)}, f32[16,16]{1,0:T(8,128)}, u32[]{:S(2)}) copy-start(f32[16,16]{1,0:T(8,128)} %param.13) | copy-start | bytes 3076
  61.0 2.0 %copy-start.18 = (f32[16,16]{1,0:T(8,128)S(1)}, f32[16,16]{1,0:T(8,128)}, u32[]{:S(2)}) copy-start(f32[16,16]{1,0:T(8,128)} %param.12) | copy-start | bytes 3076
  102.1 1.8 %copy-start.14 = (bf16[24,16,256]{2,1,0:T(8,128)(2,1)S(1)}, bf16[24,16,256]{2,1,0:T(8,128)(2,1)}, u32[]{:S(2)}) copy-start(bf16[24,16,256]{2,1,0:T(8,128)(2,1)} %get-tuple-element.55) | copy-start | bytes 589828
  102.1 1.8 %copy-start.15 = (bf16[24,16,256]{2,1,0:T(8,128)(2,1)S(1)}, bf16[24,16,256]{2,1,0:T(8,128)(2,1)}, u32[]{:S(2)}) copy-start(bf16[24,16,256]{2,1,0:T(8,128)(2,1)} %get-tuple-element.56) | copy-start | bytes 589828
  111.7 13.5 %copy-start.20 = (s32[1024]{0:T(1024)S(1)}, s32[1024]{0:T(1024)}, u32[]{:S(2)}) copy-start(s32[1024]{0:T(1024)} %param.16) | copy-start | bytes 12292
  127.0 13.3 %copy-start.2 = (f32[24,16,64]{2,1,0:T(8,128)S(1)}, f32[24,16,64]{2,1,0:T(8,128)}, u32[]{:S(2)}) copy-start(f32[24,16,64]{2,1,0:T(8,128)} %sub.91) | copy-start | bytes 294916
  127.0 13.3 %copy-start.3 = (f32[24,16,64]{2,1,0:T(8,128)S(1)}, f32[24,16,64]{2,1,0:T(8,128)}, u32[]{:S(2)}) copy-start(f32[24,16,64]{2,1,0:T(8,128)} %add.184) | copy-start | bytes 294916
  127.0 13.3 %copy-start.4 = (f32[24,16,64]{2,1,0:T(8,128)S(1)}, f32[24,16,64]{2,1,0:T(8,128)}, u32[]{:S(2)}) copy-start(f32[24,16,64]{2,1,0:T(8,128)} %sub.89) | copy-start | bytes 294916
  127.0 13.3 %copy-start.5 = (f32[24,16,64]{2,1,0:T(8,128)S(1)}, f32[24,16,64]{2,1,0:T(8,128)}, u32[]{:S(2)}) copy-start(f32[24,16,64]{2,1,0:T(8,128)} %add.180) | copy-start | bytes 294916
  127.0 13.3 %copy-start.6 = (f32[24,16,64]{2,1,0:T(8,128)S(1)}, f32[24,16,64]{2,1,0:T(8,128)}, u32[]{:S(2)}) copy-start(f32[24,16,64]{2,1,0:T(8,128)} %sub.87) | copy-start | bytes 294916
  127.0 13.3 %copy-start.7 = (f32[24,16,64]{2,1,0:T(8,128)S(1)}, f32[24,16,64]{2,1,0:T(8,128)}, u32[]{:S(2)}) copy-start(f32[24,16,64]{2,1,0:T(8,128)} %add.176) | copy-start | bytes 294916
  127.0 13.3 %copy-start.8 = (f32[24,16,64]{2,1,0:T(8,128)S(1)}, f32[24,16,64]{2,1,0:T(8,128)}, u32[]{:S(2)}) copy-start(f32[24,16,64]{2,1,0:T(8,128)} %sub.85) | copy-start | bytes 294916
  127.0 13.3 %copy-start.9 = (f32[24,16,64]{2,1,0:T(8,128)S(1)}, f32[24,16,64]{2,1,0:T(8,128)}, u32[]{:S(2)}) copy-start(f32[24,16,64]{2,1,0:T(8,128)} %add.172) | copy-start | bytes 294916
  127.1 13.3 %copy-start.10 = (f32[24,16,64]{2,1,0:T(8,128)S(1)}, f32[24,16,64]{2,1,0:T(8,128)}, u32[]{:S(2)}) copy-start(f32[24,16,64]{2,1,0:T(8,128)} %sub.83) | copy-start | bytes 294916
  127.1 13.3 %copy-start.11 = (f32[24,16,64]{2,1,0:T(8,128)S(1)}, f32[24,16,64]{2,1,0:T(8,128)}, u32[]{:S(2)}) copy-start(f32[24,16,64]{2,1,0:T(8,128)} %add.168) | copy-start | bytes 294916
  127.1 13.3 %copy-start.12 = (f32[24,16,64]{2,1,0:T(8,128)S(1)}, f32[24,16,64]{2,1,0:T(8,128)}, u32[]{:S(2)}) copy-start(f32[24,16,64]{2,1,0:T(8,128)} %sub.81) | copy-start | bytes 294916
  127.1 13.3 %copy-start.13 = (f32[24,16,64]{2,1,0:T(8,128)S(1)}, f32[24,16,64]{2,1,0:T(8,128)}, u32[]{:S(2)}) copy-start(f32[24,16,64]{2,1,0:T(8,128)} %add.164) | copy-start | bytes 294916

commit v2 on v1

--- a/solution.py
+++ b/solution.py
@@ -15,7 +15,7 @@
 GROUP_AXES = ("tile", "stn")
 
 
-def filter_dft_kernel(frames, taps, x_ref, taps_ref, ca_ref, sa_ref, cb_ref, sb_ref, out_ref, filt, table, acc):
+def filter_dft_kernel(frames, taps, x_ref, taps_ref, ca_ref, sa_ref, cb_ref, sb_ref, extra_ref, out_ref, filt, table, acc):
     step = pl.program_id(0)
     antennas = x_ref.shape[2]
     selected = cb_ref.shape[0]
@@ -57,6 +57,7 @@
 
     @pl.when(step == pl.num_programs(0) - 1)
     def _():
+        out_ref[:, 2 * rows :] = extra_ref[...]
         out_ref[:, 0:rows] = (
             acc[0:selected, 0:rows] + acc[selected : 2 * selected, rows : 2 * rows]
         ).astype(jnp.bfloat16)
@@ -71,7 +72,7 @@
     return jnp.cos(angles) * factor, jnp.sin(angles) * factor
 
 
-def channel_spectra(samples, filter_taps, channel_list):
+def channel_spectra(samples, filter_taps, channel_list, extra):
     taps, channels = filter_taps.shape
     antennas = samples.shape[0]
     selected = channel_list.shape[0]
@@ -97,16 +98,72 @@
             pl.BlockSpec((1, selected, pieces), lambda i: (i, 0, 0)),
             pl.BlockSpec((selected, LANES), lambda i: (0, 0)),
             pl.BlockSpec((selected, LANES), lambda i: (0, 0)),
+            pl.BlockSpec(extra.shape, lambda i: (0, 0)),
         ],
-        out_specs=pl.BlockSpec((selected, width), lambda i: (0, 0)),
-        out_shape=jax.ShapeDtypeStruct((selected, width), jnp.bfloat16),
+        out_specs=pl.BlockSpec((selected, width + extra.shape[1]), lambda i: (0, 0)),
+        out_shape=jax.ShapeDtypeStruct((selected, width + extra.shape[1]), jnp.bfloat16),
         scratch_shapes=[
             pltpu.VMEM((width, CHUNK), jnp.bfloat16),
             pltpu.VMEM((2 * selected, CHUNK), jnp.bfloat16),
             pltpu.VMEM((2 * selected, width), jnp.float32),
         ],
         compiler_params=pltpu.CompilerParams(vmem_limit_bytes=32 * 1024 * 1024),
-    )(x, filter_taps, ca, sa, cb, sb)
+    )(x, filter_taps, ca, sa, cb, sb, extra)
+
+
+def beam_power_kernel(frames, factor, x_ref, w_ref, mask_ref, cos_ref, sin_ref, onehot_ref, out_ref, moments):
+    share = x_ref.shape[0]
+    stations = mask_ref.shape[0]
+    pointings = onehot_ref.shape[0]
+    pairs = list(itertools.combinations(range(stations), 2))
+    for c in range(share):
+        x = x_ref[c].astype(jnp.float32)
+        real, imag = [], []
+        for s in range(stations):
+            masked = (x * mask_ref[s : s + 1, :]).astype(jnp.bfloat16)
+            terms = lax.dot_general(
+                masked, w_ref[c], (((1,), (1,)), ((), ())), preferred_element_type=jnp.float32
+            )
+            cos_part = terms[:, 0:pointings]
+            sin_part = terms[:, pointings : 2 * pointings]
+            real.append(cos_part[0:frames] + sin_part[frames : 2 * frames])
+            imag.append(cos_part[frames : 2 * frames] - sin_part[0:frames])
+        total = real[0] * real[0] + imag[0] * imag[0]
+        for s in range(1, stations):
+            total = total + (real[s] * real[s] + imag[s] * imag[s])
+        moments[0, c : c + 1, :] = jnp.sum(total, axis=0, keepdims=True) * factor
+        for i, (s, t) in enumerate(pairs):
+            even = real[s] * real[t] + imag[s] * imag[t]
+            odd = imag[s] * real[t] - real[s] * imag[t]
+            moments[1 + i, c : c + 1, :] = jnp.sum(even, axis=0, keepdims=True) * (2.0 * factor)
+            moments[1 + len(pairs) + i, c : c + 1, :] = jnp.sum(odd, axis=0, keepdims=True) * (
+                2.0 * factor
+            )
+
+    def chosen(m):
+        return jnp.dot(
+            moments[m],
+            onehot_ref[...],
+            precision=lax.Precision.HIGHEST,
+            preferred_element_type=jnp.float32,
+        )
+
+    power = chosen(0)
+    for i, (s, t) in enumerate(pairs):
+        power = power + chosen(1 + i) * (cos_ref[s] * cos_ref[t] + sin_ref[s] * sin_ref[t])
+        power = power + chosen(1 + len(pairs) + i) * (
+            sin_ref[s] * cos_ref[t] - cos_ref[s] * sin_ref[t]
+        )
+    beams = out_ref.shape[2]
+    for d in range(out_ref.shape[0]):
+        out_ref[d] = power[:, d * beams : (d + 1) * beams]
+
+
+def split_rows(values):
+    first = lax.reduce_precision(values, 8, 7)
+    second = lax.reduce_precision(values - first, 8, 7)
+    third = values - first - second
+    return jnp.stack([first, second, third], axis=1).astype(jnp.bfloat16)
 
 
 def antenna_info(antenna_tile_lag, tile_station_lag, tile_of_antenna, tile_station):
@@ -140,16 +197,18 @@
     beams = tied_beam_pointing.shape[0]
 
     info = antenna_info(antenna_tile_lag, tile_station_lag, tile_of_antenna, tile_station)
-    info = lax.all_gather(info, GROUP_AXES, axis=1, tiled=True)
-    lag = info[:pointings]
-    mask = (
-        info[pointings][None, :] == jnp.arange(stations, dtype=jnp.float32)[:, None]
-    ).astype(jnp.bfloat16)
+    info_rows = info.shape[0]
+    groups = -(-info_rows // share)
+    pieces = split_rows(info)
+    pieces = jnp.pad(pieces, ((0, groups * share - info_rows), (0, 0), (0, 0)))
+    pieces = pieces.reshape(groups, share, 3 * antennas).transpose(1, 0, 2)
+    pieces = pieces.reshape(share, groups * 3 * antennas)
+    extra_width = -(-pieces.shape[1] // LANES) * LANES
+    pieces = jnp.pad(pieces, ((0, 0), (0, extra_width - pieces.shape[1])))
+    extra = jnp.tile(pieces, (devices, 1))
 
     own_channels = lax.dynamic_slice_in_dim(channel_list, own_rank * share, share)
     omega = own_channels.astype(jnp.float32) * (TWO_PI / channels)
-    angles = lag[None] * omega[:, None, None]
-    weights = jnp.concatenate([jnp.cos(angles), jnp.sin(angles)], axis=1).astype(jnp.bfloat16)
     theta = station_beam_lag.T[:, None, :] * omega[None, :, None]
     cosine = jnp.cos(theta)
     sine = jnp.sin(theta)
@@ -157,39 +216,33 @@
         tied_beam_pointing[None, :] == jnp.arange(pointings, dtype=jnp.int32)[:, None]
     ).astype(jnp.float32)
 
-    spectra = channel_spectra(samples, filter_taps, channel_list)
+    spectra = channel_spectra(samples, filter_taps, channel_list, extra)
     spectra = lax.all_to_all(spectra, GROUP_AXES, split_axis=0, concat_axis=0, tiled=True)
-    spectra = spectra.reshape(devices, share, 2 * frames, antennas).transpose(1, 2, 0, 3)
-    spectra = spectra.reshape(share, 1, 2 * frames, devices * antennas)
-    masked = (spectra * mask[None, :, None, :]).reshape(
-        share, stations * 2 * frames, devices * antennas
-    )
-    terms = jnp.einsum("cua,cva->cuv", weights, masked, preferred_element_type=jnp.float32)
-    terms = terms.reshape(share, 2, pointings, stations, 2, frames)
-    real = terms[:, 0, :, :, 0] + terms[:, 1, :, :, 1]
-    imag = terms[:, 0, :, :, 1] - terms[:, 1, :, :, 0]
-
-    factor = 1.0 / (frames * antennas * devices)
-    pairs = list(itertools.combinations(range(stations), 2))
-    moments = [jnp.sum(real * real + imag * imag, axis=(2, 3)) * factor]
-    for s, t in pairs:
-        moments.append(
-            jnp.sum(real[:, :, s] * real[:, :, t] + imag[:, :, s] * imag[:, :, t], axis=2)
-            * (2.0 * factor)
-        )
-    for s, t in pairs:
-        moments.append(
-            jnp.sum(imag[:, :, s] * real[:, :, t] - real[:, :, s] * imag[:, :, t], axis=2)
-            * (2.0 * factor)
-        )
-    moments = jnp.stack(moments).reshape(len(moments) * share, pointings)
-    chosen = jnp.dot(moments, onehot, precision=lax.Precision.HIGHEST).reshape(-1, share, beams)
-    power = chosen[0]
-    for i, (s, t) in enumerate(pairs):
-        power = power + chosen[1 + i] * (cosine[s] * cosine[t] + sine[s] * sine[t])
-        power = power + chosen[1 + len(pairs) + i] * (sine[s] * cosine[t] - cosine[s] * sine[t])
-    power = lax.all_to_all(power, GROUP_AXES, split_axis=1, concat_axis=0, tiled=True)
-    return power.T
+    width = 2 * frames * antennas
+    total = devices * antennas
+
+    pieces = spectra[:, width : width + groups * 3 * antennas].astype(jnp.float32)
+    pieces = pieces.reshape(devices, share, groups, 3, antennas)
+    info = (pieces[:, :, :, 0] + pieces[:, :, :, 1]) + pieces[:, :, :, 2]
+    info = info.transpose(2, 1, 0, 3).reshape(groups * share, total)
+    lag = info[:pointings]
+    mask = (
+        info[pointings][None, :] == jnp.arange(stations, dtype=jnp.float32)[:, None]
+    ).astype(jnp.float32)
+    angles = lag[None] * omega[:, None, None]
+    weights = jnp.concatenate([jnp.cos(angles), jnp.sin(angles)], axis=1).astype(jnp.bfloat16)
+
+    spectra = spectra[:, :width].reshape(devices, share, 2 * frames, antennas)
+    spectra = spectra.transpose(1, 2, 0, 3).reshape(share, 2 * frames, total)
+    moment_count = stations * stations - stations + 1
+    power = pl.pallas_call(
+        functools.partial(beam_power_kernel, frames, 1.0 / (frames * total)),
+        out_shape=jax.ShapeDtypeStruct((devices, share, beams // devices), jnp.float32),
+        scratch_shapes=[pltpu.VMEM((moment_count, share, pointings), jnp.float32)],
+        compiler_params=pltpu.CompilerParams(vmem_limit_bytes=32 * 1024 * 1024),
+    )(spectra, weights, mask, cosine, sine, onehot)
+    power = lax.all_to_all(power, GROUP_AXES, split_axis=0, concat_axis=0, tiled=True)
+    return power.reshape(selected, beams // devices).T
 
 
 def solution(mesh):

time: 155 us -> 113 us (0.73)
  blocking collectives: 32.1 us -> 11.3 us
  local copies, waits for them, and re-layouts: 64.9 us -> 46.9 us
  other arithmetic: 30.1 us -> 14.8 us
  waiting for transfers between devices: 0.01 us -> 10.9 us
  Pallas kernels: 18.2 us -> 20.1 us
    all_gather x1 -> x0, blocking collectives: 22.1 us -> none  [body(): info = lax.all_gather(info, GROUP_AXES, axis=1, tiled=True)]
    reduce_sum x3 -> x0, other arithmetic: 14.3 us -> none  [the longest x2 13.3 us: body(): jnp.sum(imag[:, :, s] * real[:, :, t] - real[:, :, s] * imag[:, :, t], ax...]
    squeeze x13 -> x0, local copies, waits for them, and re-layouts: 13.4 us -> none  [the longest x6 6.45 us: body(): power = power + chosen[1 + i] * (cosine[s] * cosine[t] + sine[s] * sine[t])]
    all_to_all x1, waiting for transfers between devices: 0.01 us -> 10.9 us  [body(): lax.all_to_all(spectra, GROUP_AXES, split_axis=0, concat_axis=0, tiled=True)]
    add x7 -> x0, local copies, waits for them, and re-layouts: 4.68 us -> none  [the longest x6 4.61 us: body(): power = power + chosen[1 + i] * (cosine[s] * cosine[t] + sine[s] * sine[t])]
    sub x6 -> x0, local copies, waits for them, and re-layouts: 4.59 us -> none  [body(): sine[s] * cosine[t] - cosine[s] * sine[t]]
    unnamed x48 -> x23, local copies, waits for them, and re-layouts: 3.65 us -> 7.47 us
    pallas_call x0 -> x1, Pallas kernels: none -> 2.61 us  [body(): pl.pallas_call(functools.partial(beam_power_kernel, frames, 1.0 / (frames...]
  transfers between devices with their start and end apart: 1 -> 1, of which waited for: 0 -> 1; matrix products, arithmetic and copies ran while one was open for 9% -> 3% of each run, Pallas kernels for 0% -> 0%
where the time goes in v2:
time: 113 us; the launch traced here: 112 us
  local copies, waits for them, and re-layouts  46.9 us (42%)
  Pallas kernels  20.1 us (18%)
  other arithmetic  14.8 us (13%)
  blocking collectives  11.3 us (10%)
  waiting for transfers between devices  10.9 us (10%)
  starting transfers between devices  7.4 us (7%)
    reshape x2, local copies, waits for them, and re-layouts, channel_spectra(): x = samples.reshape(antennas, 2, blocks, channels).transpose(2, 1, 0, 3)  24.9 us
    pallas_call x1, Pallas kernels, channel_spectra(): pl.pallas_call(functools.partial(filter_dft_kernel, frames, taps), grid=(...  17.5 us
    all_to_all x1, blocking collectives, body(): lax.all_to_all(power, GROUP_AXES, split_axis=0, concat_axis=0, tiled=True)  11.3 us
    all_to_all x1, waiting for transfers between devices, body(): lax.all_to_all(spectra, GROUP_AXES, split_axis=0, concat_axis=0, tiled=True)  10.9 us
    unnamed x23, local copies, waits for them, and re-layouts  7.47 us
    all_to_all x1, starting transfers between devices, body(): lax.all_to_all(spectra, GROUP_AXES, split_axis=0, concat_axis=0, tiled=True)  7.4 us
    mul x1, other arithmetic, unit_tables(): return (jnp.cos(angles) * factor, jnp.sin(angles) * factor)  7.38 us
    transpose x1, local copies, waits for them, and re-layouts, body(): spectra = spectra.transpose(1, 2, 0, 3).reshape(share, 2 * frames, total)  4.67 us
  transfers between devices with their start and end apart: 1, of which 1 were waited for; matrix products, arithmetic and copies ran while one was open for 3% of the time, Pallas kernels for 0%

profile of v2, /device:TPU:0, one launch (start us, length us, event | category | flops | bytes accessed | tf_op | source)
XLA Modules:
  0.0 111.6 jit_solution(16609529733472874748)
XLA Ops:
  0.0 13.8 %reshape.207 = bf16[16,2,31,4096]{3,2,1,0:T(8,128)(2,1)} reshape(bf16[16,2,126976]{2,1,0:T(2,128)(2,1)} %param.9) | data formatting | bytes 16252928 | tf_op jit(solution)/shard_map/reshape | solution.py:83
  13.8 0.0 copy-start.4
  13.8 11.1 %copy.64 = bf16[16,2,31,4096]{3,0,1,2:T(8,128)(2,1)} copy(bf16[16,2,31,4096]{3,2,1,0:T(8,128)(2,1)} %reshape.207) | data formatting | bytes 16252928 | tf_op jit(solution)/shard_map/reshape | solution.py:83
  24.9 0.0 copy-done.4
  24.9 0.8 fusion.9
  25.8 0.1 fusion.12
  25.9 1.7 %copy.47 = f32[8,384,4]{2,1,0:T(8,128)} copy(f32[8,384,4]{1,0,2:T(8,128)S(1)} %fusion.12) | data formatting | bytes 98304 | tf_op jit(solution)/shard_map/convert_element_type | solution.py:71
  27.5 0.0 copy-start.7
  27.5 0.0 copy-start.8
  27.5 0.0 copy-start.6
  27.5 0.0 copy-start.5
  27.6 7.4 %sine_multiply_fusion = (f32[8,384,4]{2,1,0:T(8,128)S(1)}, f32[8,384,4]{2,1,0:T(8,128)S(1)}) fusion(f32[8,384,4]{2,1,0:T(8,128)} %copy.47), kind=kLoop, calls=%fused_computation.1 | loop fusion | flops 36864 | bytes 147456 | tf_op jit(solution)/shard_map/mul | solution.py:72
  34.9 0.0 copy-done.7
  34.9 0.1 iota_compare_fusion.1
  35.0 0.0 copy-done.8
  35.0 0.2 select_reduce_fusion.1
  35.2 0.0 copy-done.6
  35.2 0.1 select_reduce_fusion
  35.3 0.0 copy-done.5
  35.4 0.6 pad_maximum_fusion.1
  36.0 1.4 %copy.61 = bf16[17,3,16]{0,2,1:T(8,128)(2,1)} copy(bf16[17,3,16]{2,0,1:T(8,128)(2,1)} %pad_maximum_fusion.1) | data formatting | bytes 3264
  37.4 0.7 pad.8.clone
  38.1 0.7 copy.62
  38.8 0.7 pad.9.clone
  39.5 0.0 copy-start
  39.5 3.3 %copy-done = bf16[16,2,31,4096]{3,0,1,2:T(8,128)(2,1)S(1)} copy-done((bf16[16,2,31,4096]{3,0,1,2:T(8,128)(2,1)S(1)}, bf16[16,2,31,4096]{3,0,1,2:T(8,128)(2,1)}, u32[]{:S(2)}) %copy-start) | copy-done | bytes 8126488
  42.8 0.0 copy-start.2
  42.8 0.9 copy-done.2
  43.8 0.0 copy-start.3
  43.8 17.5 %shard_map.91 = bf16[384,640]{1,0:T(8,128)(2,1)S(1)} custom-call(bf16[31,2,16,4096]{3,2,1,0:T(8,128)(2,1)S(1)} %bitcast.31, f32[16,4096]{1,0:T(8,128)S(1)} %copy-done.2, f32[8,384,4]{2,1,0:T(8,128)S(1)} %get-tuple-element.6.ca_ref, f32[8,384,4]{2,1,0:T(8,128)S(1)} %get-tuple-element.5.sa_ref, f32[384,128]{1,0:T(8,128)S(1)} %get-tuple-element.15.cb_ref, ...), custom_call_target="tpu_custom_call" | custom-call | tf_op jit(solution)/shard_map/pallas_call | solution.py:91
  61.3 0.0 copy-start.1
  61.3 0.8 copy-done.1
  62.1 7.4 %all-to-all-start = ((bf16[16,24,640]{2,1,0:T(8,128)(2,1)}), bf16[16,24,640]{2,1,0:T(8,128)(2,1)S(1)}, u32[]{:S(2)}, u32[]{:S(2)}) async-start(bf16[16,24,640]{2,1,0:T(8,128)(2,1)} %bitcast.32), calls=%async_computation | async-start | bytes 983040 | tf_op jit(solution)/shard_map/all_to_all | solution.py:220
  69.5 0.8 convert_multiply_fusion
  70.2 0.7 fusion.11.onehot_ref
  70.9 0.0 copy-done.3
  70.9 1.4 %multiply_sine_fusion = (f32[4,24,1024]{2,1,0:T(8,128)S(1)}, f32[4,24,1024]{2,1,0:T(8,128)S(1)}) fusion(f32[24]{0:T(128)S(1)} %convert_multiply_fusion, f32[4,1024]{1,0:T(4,128)S(1)} %bitcast.41), kind=kLoop, calls=%fused_computation.3 | loop fusion | flops 98304 | bytes 802912 | tf_op jit(solution)/shard_map/sin | solution.py:214
  72.4 10.9 %all-to-all-done = bf16[16,24,640]{2,1,0:T(8,128)(2,1)S(1)} async-done(((bf16[16,24,640]{2,1,0:T(8,128)(2,1)}), bf16[16,24,640]{2,1,0:T(8,128)(2,1)S(1)}, u32[]{:S(2)}, u32[]{:S(2)}) %all-to-all-start) | async-done | bytes 491552 | tf_op jit(solution)/shard_map/all_to_all | solution.py:220
  83.3 0.2 copy.51
  83.5 2.7 %reshape.200 = bf16[16,24,32,16]{1,0,3,2:T(8,128)(2,1)S(1)} reshape(bf16[384,512]{0,1:T(8,128)(2,1)S(1)} %copy.51) | data formatting | bytes 786432 | tf_op jit(solution)/shard_map/reshape | solution.py:235
  86.2 4.7 %copy.52 = bf16[24,32,16,16]{1,3,2,0:T(8,128)(2,1)} copy(bf16[24,32,16,16]{0,2,3,1:T(8,128)(2,1)S(1)} %bitcast.34) | data formatting | bytes 786432 | tf_op jit(solution)/shard_map/transpose | solution.py:236
  90.9 1.6 %copy.56.x_ref = bf16[24,32,256]{2,1,0:T(8,128)(2,1)S(1)} copy(bf16[24,32,256]{1,2,0:T(8,128)(2,1)} %bitcast.35) | data formatting | bytes 786432 | tf_op jit(solution)/shard_map/reshape | solution.py:236
  92.5 0.1 copy.60
  92.6 0.3 reshape.206
  92.9 0.1 slice.36
  93.0 0.1 copy.54
  93.2 0.1 mul.103
  93.3 1.7 %fusion = (bf16[24,16,256]{2,1,0:T(8,128)(2,1)S(1)}, bf16[24,16,256]{2,1,0:T(8,128)(2,1)S(1)}) fusion(f32[24]{0:T(128)S(1)} %convert_multiply_fusion, f32[16,256]{1,0:T(8,128)S(1)} %mul.103), kind=kLoop, calls=%fused_computation.7 | loop fusion | flops 294912 | bytes 409696 | tf_op jit(solution)/shard_map/convert.1
  95.0 0.2 copy.55
  95.2 0.1 eq.52
  95.3 2.6 %shard_map.92 = f32[16,24,64]{2,1,0:T(8,128)S(1)} custom-call(bf16[24,32,256]{2,1,0:T(8,128)(2,1)S(1)} %copy.56.x_ref, bf16[24,32,256]{2,1,0:T(8,128)(2,1)S(1)} %pad_maximum_fusion.w_ref, f32[4,256]{1,0:T(4,128)S(1)} %fusion.15.mask_ref, f32[4,24,1024]{2,1,0:T(8,128)S(1)} %get-tuple-element.8.cos_ref, f32[4,24,1024]{2,1,0:T(8,128)S(1)} %get-tuple-element.7.sin_ref, ...), custom_call_target="tpu_custom_call" | custom-call | tf_op jit(solution)/shard_map/pallas_call | solution.py:238
  97.9 0.2 reshape.208
  98.1 11.3 %all_to_all.17 = f32[16,1,1536]{2,1,0:T(1,128)S(1)} all-to-all(f32[16,1,1536]{2,1,0:T(1,128)S(1)} %reshape.208), channel_id=1, replica_groups=mesh['grp'=2,'tile'=8,'stn'=2] {'tile','stn'}, dimensions={0} | all-to-all | bytes 196608 | tf_op jit(solution)/shard_map/all_to_all | solution.py:244
  109.4 0.5 broadcast.101
  109.9 0.9 reduce
  110.8 0.1 reshape.209
  110.9 0.8 copy.57
  (10 shorter events, 0.2 us)
Async XLA Ops:
  13.8 11.1 %copy-start.4 = (s32[384]{0:T(512)S(1)}, s32[384]{0:T(512)}, u32[]{:S(2)}) copy-start(s32[384]{0:T(512)} %param.11) | copy-start | bytes 4612
  27.5 7.4 %copy-start.7 = (s32[16]{0:T(128)S(1)}, s32[16]{0:T(128)}, u32[]{:S(2)}) copy-start(s32[16]{0:T(128)} %param.14) | copy-start | bytes 196
  27.5 7.5 %copy-start.8 = (s32[16]{0:T(128)S(1)}, s32[16]{0:T(128)}, u32[]{:S(2)}) copy-start(s32[16]{0:T(128)} %param.15) | copy-start | bytes 196
  27.5 7.7 %copy-start.6 = (f32[16,16]{1,0:T(8,128)S(1)}, f32[16,16]{1,0:T(8,128)}, u32[]{:S(2)}) copy-start(f32[16,16]{1,0:T(8,128)} %param.13) | copy-start | bytes 3076
  27.5 7.8 %copy-start.5 = (f32[16,16]{1,0:T(8,128)S(1)}, f32[16,16]{1,0:T(8,128)}, u32[]{:S(2)}) copy-start(f32[16,16]{1,0:T(8,128)} %param.12) | copy-start | bytes 3076
  39.5 3.3 %copy-start = (bf16[16,2,31,4096]{3,0,1,2:T(8,128)(2,1)S(1)}, bf16[16,2,31,4096]{3,0,1,2:T(8,128)(2,1)}, u32[]{:S(2)}) copy-start(bf16[16,2,31,4096]{3,0,1,2:T(8,128)(2,1)} %copy.64) | copy-start | bytes 24379396
  42.8 0.9 copy-start.2
  43.8 27.2 %copy-start.3 = (f32[1024,4]{0,1:T(4,128)S(1)}, f32[1024,4]{0,1:T(4,128)}, u32[]{:S(2)}) copy-start(f32[1024,4]{0,1:T(4,128)} %param.17) | copy-start | bytes 49156
  61.3 0.8 copy-start.1
  62.1 21.2 %all-to-all-start = ((bf16[16,24,640]{2,1,0:T(8,128)(2,1)}), bf16[16,24,640]{2,1,0:T(8,128)(2,1)S(1)}, u32[]{:S(2)}, u32[]{:S(2)}) async-start(bf16[16,24,640]{2,1,0:T(8,128)(2,1)} %bitcast.32), calls=%async_computation | async-start | bytes 983040 | tf_op jit(solution)/shard_map/all_to_all | solution.py:220

commit v3 on v2

--- a/solution.py
+++ b/solution.py
@@ -17,7 +17,7 @@
 
 def filter_dft_kernel(frames, taps, x_ref, taps_ref, ca_ref, sa_ref, cb_ref, sb_ref, extra_ref, out_ref, filt, table, acc):
     step = pl.program_id(0)
-    antennas = x_ref.shape[2]
+    antennas = x_ref.shape[0]
     selected = cb_ref.shape[0]
     rows = frames * antennas
 
@@ -34,7 +34,7 @@
         ]
         for r in range(2):
             blocks = [
-                x_ref[k, r, :, lanes].astype(jnp.float32) for k in range(frames + taps - 1)
+                x_ref[:, k, r, lanes].astype(jnp.float32) for k in range(frames + taps - 1)
             ]
             for f in range(frames):
                 total = blocks[f] * weights[0]
@@ -80,7 +80,7 @@
     frames = blocks - taps + 1
     steps = channels // CHUNK
     pieces = CHUNK // LANES
-    x = samples.reshape(antennas, 2, blocks, channels).transpose(2, 1, 0, 3)
+    x = samples.reshape(antennas, 2, blocks, channels).transpose(0, 2, 1, 3)
     coarse = lax.broadcasted_iota(jnp.int32, (selected, channels // LANES), 1) * LANES
     fine = lax.broadcasted_iota(jnp.int32, (selected, LANES), 1)
     ca, sa = unit_tables(coarse, channel_list, channels, 1.0 / math.sqrt(channels))
@@ -92,7 +92,7 @@
         functools.partial(filter_dft_kernel, frames, taps),
         grid=(steps,),
         in_specs=[
-            pl.BlockSpec((blocks, 2, antennas, CHUNK), lambda i: (0, 0, 0, i)),
+            pl.BlockSpec((antennas, blocks, 2, CHUNK), lambda i: (0, 0, 0, i)),
             pl.BlockSpec((taps, CHUNK), lambda i: (0, i)),
             pl.BlockSpec((1, selected, pieces), lambda i: (i, 0, 0)),
             pl.BlockSpec((1, selected, pieces), lambda i: (i, 0, 0)),

time: 113 us -> 110 us (0.973)
  local copies, waits for them, and re-layouts: 46.9 us -> 22 us
  Pallas kernels: 20.1 us -> 41.3 us
  other arithmetic: 14.8 us -> 16.2 us
    reshape x2 -> x0, local copies, waits for them, and re-layouts: 24.9 us -> none  [channel_spectra(): x = samples.reshape(antennas, 2, blocks, channels).transpose(2, 1, 0, 3)]
    pallas_call x1, Pallas kernels: 17.5 us -> 38.7 us  [channel_spectra(): pl.pallas_call(functools.partial(filter_dft_kernel, frames, taps), grid=(...]
    unnamed x23 -> x25, local copies, waits for them, and re-layouts: 7.47 us -> 7.48 us
where the time goes in v3:
time: 110 us; the launch traced here: 109 us
  Pallas kernels  41.3 us (38%)
  local copies, waits for them, and re-layouts  22 us (20%)
  other arithmetic  16.2 us (15%)
  blocking collectives  11.3 us (10%)
  waiting for transfers between devices  10.9 us (10%)
  starting transfers between devices  7.39 us (7%)
    pallas_call x1, Pallas kernels, channel_spectra(): pl.pallas_call(functools.partial(filter_dft_kernel, frames, taps), grid=(...  38.7 us
    all_to_all x1, blocking collectives, body(): lax.all_to_all(power, GROUP_AXES, split_axis=0, concat_axis=0, tiled=True)  11.3 us
    all_to_all x1, waiting for transfers between devices, body(): lax.all_to_all(spectra, GROUP_AXES, split_axis=0, concat_axis=0, tiled=True)  10.9 us
    unnamed x25, local copies, waits for them, and re-layouts  7.48 us
    all_to_all x1, starting transfers between devices, body(): lax.all_to_all(spectra, GROUP_AXES, split_axis=0, concat_axis=0, tiled=True)  7.39 us
    mul x1, other arithmetic, unit_tables(): return (jnp.cos(angles) * factor, jnp.sin(angles) * factor)  7.38 us
    transpose x1, local copies, waits for them, and re-layouts, body(): spectra = spectra.transpose(1, 2, 0, 3).reshape(share, 2 * frames, total)  4.69 us
    reshape x1, local copies, waits for them, and re-layouts, body(): spectra = spectra[:, :width].reshape(devices, share, 2 * frames, antennas)  2.73 us
  transfers between devices with their start and end apart: 1, of which 1 were waited for; matrix products, arithmetic and copies ran while one was open for 3% of the time, Pallas kernels for 0%

profile of v3, /device:TPU:0, one launch (start us, length us, event | category | flops | bytes accessed | tf_op | source)
XLA Modules:
  0.0 109.3 jit_solution(1402281738879229353)
XLA Ops:
  0.0 1.5 %fusion.9 = (f32[384,128]{1,0:T(8,128)S(1)}, f32[384,128]{1,0:T(8,128)S(1)}) fusion(s32[384]{0:T(512)} %param.11), kind=kLoop, calls=%fused_computation.22 | loop fusion | flops 688128 | bytes 394752 | tf_op jit(solution)/shard_map/sin | solution.py:72
  1.5 0.8 fusion.12
  2.3 1.7 %copy.39 = f32[8,384,4]{2,1,0:T(8,128)} copy(f32[8,384,4]{1,0,2:T(8,128)S(1)} %fusion.12) | data formatting | bytes 98304 | tf_op jit(solution)/shard_map/convert_element_type | solution.py:71
  4.0 0.0 copy-start.8
  4.0 0.0 copy-start.9
  4.0 0.0 copy-start.5
  4.0 0.0 copy-start.4
  4.0 7.4 %sine_multiply_fusion = (f32[8,384,4]{2,1,0:T(8,128)S(1)}, f32[8,384,4]{2,1,0:T(8,128)S(1)}) fusion(f32[8,384,4]{2,1,0:T(8,128)} %copy.39), kind=kLoop, calls=%fused_computation | loop fusion | flops 36864 | bytes 147456 | tf_op jit(solution)/shard_map/mul | solution.py:72
  11.4 0.0 copy-done.8
  11.4 0.1 iota_compare_fusion.1
  11.5 0.0 copy-done.9
  11.5 0.2 select_reduce_fusion.1
  11.6 0.0 copy-done.5
  11.7 0.1 select_reduce_fusion
  11.8 0.0 copy-done.4
  11.8 0.6 pad_maximum_fusion.1
  12.4 1.4 %copy.51 = bf16[17,3,16]{0,2,1:T(8,128)(2,1)} copy(bf16[17,3,16]{2,0,1:T(8,128)(2,1)} %pad_maximum_fusion.1) | data formatting | bytes 3264
  13.8 0.7 pad.8.clone
  14.5 0.7 copy.52
  15.2 0.7 pad.9.clone
  15.9 0.0 copy-start
  16.0 3.3 %copy-done = bf16[16,2,126976]{2,1,0:T(2,128)(2,1)S(1)} copy-done((bf16[16,2,126976]{2,1,0:T(2,128)(2,1)S(1)}, bf16[16,2,126976]{2,1,0:T(2,128)(2,1)}, u32[]{:S(2)}) %copy-start) | copy-done | bytes 8126488
  19.3 0.0 copy-start.2
  19.3 0.9 copy-done.2
  20.2 0.0 copy-start.3
  20.2 38.7 %shard_map.91 = bf16[384,640]{1,0:T(8,128)(2,1)S(1)} custom-call(bf16[16,31,2,4096]{3,2,1,0:T(2,128)(2,1)S(1)} %bitcast.31, f32[16,4096]{1,0:T(8,128)S(1)} %copy-done.2, f32[8,384,4]{2,1,0:T(8,128)S(1)} %get-tuple-element.6.ca_ref, f32[8,384,4]{2,1,0:T(8,128)S(1)} %get-tuple-element.5.sa_ref, f32[384,128]{1,0:T(8,128)S(1)} %get-tuple-element.15.cb_ref, ...), custom_call_target="tpu_custom_call" | custom-call | tf_op jit(solution)/shard_map/pallas_call | solution.py:91
  58.9 0.0 copy-start.1
  58.9 0.8 copy-done.1
  59.7 7.4 %all-to-all-start = ((bf16[16,24,640]{2,1,0:T(8,128)(2,1)}), bf16[16,24,640]{2,1,0:T(8,128)(2,1)S(1)}, u32[]{:S(2)}, u32[]{:S(2)}) async-start(bf16[16,24,640]{2,1,0:T(8,128)(2,1)} %bitcast.32), calls=%async_computation | async-start | bytes 983040 | tf_op jit(solution)/shard_map/all_to_all | solution.py:220
  67.1 0.8 convert_multiply_fusion
  67.9 0.0 copy-start.6
  67.9 0.7 fusion.11.onehot_ref
  68.6 0.0 copy-done.3
  68.6 1.4 %multiply_sine_fusion = (f32[4,24,1024]{2,1,0:T(8,128)S(1)}, f32[4,24,1024]{2,1,0:T(8,128)S(1)}) fusion(f32[24]{0:T(128)S(1)} %convert_multiply_fusion, f32[4,1024]{1,0:T(4,128)S(1)} %bitcast.41), kind=kLoop, calls=%fused_computation.2 | loop fusion | flops 98304 | bytes 802912 | tf_op jit(solution)/shard_map/sin | solution.py:214
  70.0 10.9 %all-to-all-done = bf16[16,24,640]{2,1,0:T(8,128)(2,1)S(1)} async-done(((bf16[16,24,640]{2,1,0:T(8,128)(2,1)}), bf16[16,24,640]{2,1,0:T(8,128)(2,1)S(1)}, u32[]{:S(2)}, u32[]{:S(2)}) %all-to-all-start) | async-done | bytes 491552 | tf_op jit(solution)/shard_map/all_to_all | solution.py:220
  80.9 0.0 copy-done.6
  80.9 0.2 copy.43
  81.2 2.7 %reshape.200 = bf16[16,24,32,16]{1,0,3,2:T(8,128)(2,1)S(1)} reshape(bf16[384,512]{0,1:T(8,128)(2,1)S(1)} %copy.43) | data formatting | bytes 786432 | tf_op jit(solution)/shard_map/reshape | solution.py:235
  83.9 4.7 %copy.44 = bf16[24,32,16,16]{1,3,2,0:T(8,128)(2,1)} copy(bf16[24,32,16,16]{0,2,3,1:T(8,128)(2,1)S(1)} %bitcast.34) | data formatting | bytes 786432 | tf_op jit(solution)/shard_map/transpose | solution.py:236
  88.6 0.0 copy-start.7
  88.6 1.6 %copy.48.x_ref = bf16[24,32,256]{2,1,0:T(8,128)(2,1)S(1)} copy(bf16[24,32,256]{1,2,0:T(8,128)(2,1)} %bitcast.35) | data formatting | bytes 786432 | tf_op jit(solution)/shard_map/reshape | solution.py:236
  90.2 0.1 copy.50
  90.3 0.3 reshape.206
  90.6 0.1 slice.36
  90.7 0.1 copy.46
  90.9 0.1 mul.103
  91.0 0.0 copy-done.7
  91.0 1.7 %fusion = (bf16[24,16,256]{2,1,0:T(8,128)(2,1)S(1)}, bf16[24,16,256]{2,1,0:T(8,128)(2,1)S(1)}) fusion(f32[24]{0:T(128)S(1)} %copy-done.7, f32[16,256]{1,0:T(8,128)S(1)} %mul.103), kind=kLoop, calls=%fused_computation.6 | loop fusion | flops 294912 | bytes 409696 | tf_op jit(solution)/shard_map/convert.1
  92.7 0.2 copy.47
  92.9 0.1 eq.52
  93.0 2.6 %shard_map.92 = f32[16,24,64]{2,1,0:T(8,128)S(1)} custom-call(bf16[24,32,256]{2,1,0:T(8,128)(2,1)S(1)} %copy.48.x_ref, bf16[24,32,256]{2,1,0:T(8,128)(2,1)S(1)} %pad_maximum_fusion.w_ref, f32[4,256]{1,0:T(4,128)S(1)} %fusion.15.mask_ref, f32[4,24,1024]{2,1,0:T(8,128)S(1)} %get-tuple-element.8.cos_ref, f32[4,24,1024]{2,1,0:T(8,128)S(1)} %get-tuple-element.7.sin_ref, ...), custom_call_target="tpu_custom_call" | custom-call | tf_op jit(solution)/shard_map/pallas_call | solution.py:238
  95.6 0.2 reshape.207
  95.8 11.3 %all_to_all.17 = f32[16,1,1536]{2,1,0:T(1,128)S(1)} all-to-all(f32[16,1,1536]{2,1,0:T(1,128)S(1)} %reshape.207), channel_id=1, replica_groups=mesh['grp'=2,'tile'=8,'stn'=2] {'tile','stn'}, dimensions={0} | all-to-all | bytes 196608 | tf_op jit(solution)/shard_map/all_to_all | solution.py:244
  107.1 0.5 broadcast.101
  107.6 0.9 reduce
  108.5 0.1 reshape.208
  108.6 0.8 copy.49
  (10 shorter events, 0.2 us)
Async XLA Ops:
  4.0 7.4 %copy-start.8 = (s32[16]{0:T(128)S(1)}, s32[16]{0:T(128)}, u32[]{:S(2)}) copy-start(s32[16]{0:T(128)} %param.14) | copy-start | bytes 196
  4.0 7.5 %copy-start.9 = (s32[16]{0:T(128)S(1)}, s32[16]{0:T(128)}, u32[]{:S(2)}) copy-start(s32[16]{0:T(128)} %param.15) | copy-start | bytes 196
  4.0 7.7 %copy-start.5 = (f32[16,16]{1,0:T(8,128)S(1)}, f32[16,16]{1,0:T(8,128)}, u32[]{:S(2)}) copy-start(f32[16,16]{1,0:T(8,128)} %param.13) | copy-start | bytes 3076
  4.0 7.8 %copy-start.4 = (f32[16,16]{1,0:T(8,128)S(1)}, f32[16,16]{1,0:T(8,128)}, u32[]{:S(2)}) copy-start(f32[16,16]{1,0:T(8,128)} %param.12) | copy-start | bytes 3076
  15.9 3.3 %copy-start = (bf16[16,2,126976]{2,1,0:T(2,128)(2,1)S(1)}, bf16[16,2,126976]{2,1,0:T(2,128)(2,1)}, u32[]{:S(2)}) copy-start(bf16[16,2,126976]{2,1,0:T(2,128)(2,1)} %param.9) | copy-start | bytes 24379396
  19.3 0.9 copy-start.2
  20.2 48.4 %copy-start.3 = (f32[1024,4]{0,1:T(4,128)S(1)}, f32[1024,4]{0,1:T(4,128)}, u32[]{:S(2)}) copy-start(f32[1024,4]{0,1:T(4,128)} %param.17) | copy-start | bytes 49156
  58.9 0.8 copy-start.1
  59.7 21.2 %all-to-all-start = ((bf16[16,24,640]{2,1,0:T(8,128)(2,1)}), bf16[16,24,640]{2,1,0:T(8,128)(2,1)S(1)}, u32[]{:S(2)}, u32[]{:S(2)}) async-start(bf16[16,24,640]{2,1,0:T(8,128)(2,1)} %bitcast.32), calls=%async_computation | async-start | bytes 983040 | tf_op jit(solution)/shard_map/all_to_all | solution.py:220
  67.9 13.0 %copy-start.6 = (f32[24]{0:T(128)}, f32[24]{0:T(128)S(1)}, u32[]{:S(2)}) copy-start(f32[24]{0:T(128)S(1)} %convert_multiply_fusion) | copy-start | bytes 292
  88.6 2.4 %copy-start.7 = (f32[24]{0:T(128)S(1)}, f32[24]{0:T(128)}, u32[]{:S(2)}) copy-start(f32[24]{0:T(128)} %copy-done.6) | copy-start | bytes 292

commit v4 on v3

--- a/solution.py
+++ b/solution.py
@@ -85,6 +85,7 @@
     fine = lax.broadcasted_iota(jnp.int32, (selected, LANES), 1)
     ca, sa = unit_tables(coarse, channel_list, channels, 1.0 / math.sqrt(channels))
     cb, sb = unit_tables(fine, channel_list, channels, 1.0)
+    ca, sa, cb, sb = lax.optimization_barrier((ca, sa, cb, sb))
     ca = ca.reshape(selected, steps, pieces).transpose(1, 0, 2)
     sa = sa.reshape(selected, steps, pieces).transpose(1, 0, 2)
     width = 2 * frames * antennas

time: 110 us -> 106 us (0.964)
  other arithmetic: 16.2 us -> 11 us
    mul x1, other arithmetic: 7.38 us -> 0.96 us  [unit_tables(): return (jnp.cos(angles) * factor, jnp.sin(angles) * factor)]
    reshape x0 -> x4, local copies, waits for them, and re-layouts: none -> 2.45 us  [the longest x2 1.94 us: channel_spectra(): sa = sa.reshape(selected, steps, pieces).transpose(1, 0, 2)]
    convert_element_type x1 -> x0, local copies, waits for them, and re-layouts: 1.66 us -> none  [unit_tables(): angles = turn_count.astype(jnp.float32) * (TWO_PI / channels)]
    unnamed x25 -> x19, local copies, waits for them, and re-layouts: 7.48 us -> 7.47 us
where the time goes in v4:
time: 106 us; the launch traced here: 105 us
  Pallas kernels  41.3 us (39%)
  local copies, waits for them, and re-layouts  22.7 us (21%)
  blocking collectives  11.3 us (11%)
  other arithmetic  11 us (10%)
  waiting for transfers between devices  10.9 us (10%)
  starting transfers between devices  7.4 us (7%)
    pallas_call x1, Pallas kernels, channel_spectra(): pl.pallas_call(functools.partial(filter_dft_kernel, frames, taps), grid=(...  38.7 us
    all_to_all x1, blocking collectives, body(): lax.all_to_all(power, GROUP_AXES, split_axis=0, concat_axis=0, tiled=True)  11.3 us
    all_to_all x1, waiting for transfers between devices, body(): lax.all_to_all(spectra, GROUP_AXES, split_axis=0, concat_axis=0, tiled=True)  10.9 us
    unnamed x19, local copies, waits for them, and re-layouts  7.47 us
    all_to_all x1, starting transfers between devices, body(): lax.all_to_all(spectra, GROUP_AXES, split_axis=0, concat_axis=0, tiled=True)  7.4 us
    transpose x1, local copies, waits for them, and re-layouts, body(): spectra = spectra.transpose(1, 2, 0, 3).reshape(share, 2 * frames, total)  4.61 us
    reshape x1, local copies, waits for them, and re-layouts, body(): spectra = spectra[:, :width].reshape(devices, share, 2 * frames, antennas)  2.73 us
    pallas_call x1, Pallas kernels, body(): pl.pallas_call(functools.partial(beam_power_kernel, frames, 1.0 / (frames...  2.61 us
  transfers between devices with their start and end apart: 1, of which 1 were waited for; matrix products, arithmetic and copies ran while one was open for 3% of the time, Pallas kernels for 0%

profile of v4, /device:TPU:0, one launch (start us, length us, event | category | flops | bytes accessed | tf_op | source)
XLA Modules:
  0.0 104.9 jit_solution(13917213671322976454)
XLA Ops:
  0.0 1.5 %fusion.9 = (f32[384,128]{1,0:T(8,128)S(1)}, f32[384,128]{1,0:T(8,128)S(1)}) fusion(s32[384]{0:T(512)} %param.11), kind=kLoop, calls=%fused_computation.20 | loop fusion | flops 688128 | bytes 394752 | tf_op jit(solution)/shard_map/sin | solution.py:72
  1.5 1.0 sine_multiply_fusion
  2.5 0.0 copy-start.6
  2.5 0.0 copy-start.5
  2.5 0.5 copy.45
  3.0 0.6 reshape.187
  3.7 1.3 %copy.46 = f32[384,8,4]{2,0,1:T(8,128)S(1)} copy(f32[384,8,4]{0,2,1:T(4,128)} %reshape.187) | data formatting | bytes 98304 | tf_op jit(solution)/shard_map/reshape | solution.py:90
  5.0 0.7 iota_compare_fusion.1
  5.7 0.9 select_reduce_fusion.1
  6.6 0.0 copy-done.6
  6.6 0.1 select_reduce_fusion
  6.7 0.0 copy-done.5
  6.7 0.6 pad_maximum_fusion.1
  7.4 1.4 %copy.58 = bf16[17,3,16]{0,2,1:T(8,128)(2,1)} copy(bf16[17,3,16]{2,0,1:T(8,128)(2,1)} %pad_maximum_fusion.1) | data formatting | bytes 3264
  8.8 0.7 pad.8.clone
  9.5 0.7 copy.59
  10.2 0.7 pad.9.clone
  10.9 0.0 copy-start
  10.9 3.3 %copy-done = bf16[16,2,126976]{2,1,0:T(2,128)(2,1)S(1)} copy-done((bf16[16,2,126976]{2,1,0:T(2,128)(2,1)S(1)}, bf16[16,2,126976]{2,1,0:T(2,128)(2,1)}, u32[]{:S(2)}) %copy-start) | copy-done | bytes 8126488
  14.2 0.0 copy-start.2
  14.2 0.9 copy-done.2
  15.1 0.0 copy-start.4
  15.1 38.7 %shard_map.91 = bf16[384,640]{1,0:T(8,128)(2,1)S(1)} custom-call(bf16[16,31,2,4096]{3,2,1,0:T(2,128)(2,1)S(1)} %bitcast.37, f32[16,4096]{1,0:T(8,128)S(1)} %copy-done.2, f32[8,384,4]{2,1,0:T(8,128)S(1)} %bitcast.38, f32[8,384,4]{2,1,0:T(8,128)S(1)} %bitcast.39, f32[384,128]{1,0:T(8,128)S(1)} %get-tuple-element.11.cb_ref, ...), custom_call_target="tpu_custom_call" | custom-call | tf_op jit(solution)/shard_map/pallas_call | solution.py:92
  53.9 0.0 copy-start.1
  53.9 0.8 copy-done.1
  54.7 7.4 %all-to-all-start = ((bf16[16,24,640]{2,1,0:T(8,128)(2,1)}), bf16[16,24,640]{2,1,0:T(8,128)(2,1)S(1)}, u32[]{:S(2)}, u32[]{:S(2)}) async-start(bf16[16,24,640]{2,1,0:T(8,128)(2,1)} %bitcast.40), calls=%async_computation | async-start | bytes 983040 | tf_op jit(solution)/shard_map/all_to_all | solution.py:221
  62.1 0.8 convert_multiply_fusion
  62.8 0.7 fusion.11.onehot_ref
  63.5 0.0 copy-done.4
  63.5 1.4 %multiply_sine_fusion = (f32[4,24,1024]{2,1,0:T(8,128)S(1)}, f32[4,24,1024]{2,1,0:T(8,128)S(1)}) fusion(f32[24]{0:T(128)S(1)} %convert_multiply_fusion, f32[4,1024]{1,0:T(4,128)S(1)} %bitcast.49), kind=kLoop, calls=%fused_computation | loop fusion | flops 98304 | bytes 802912 | tf_op jit(solution)/shard_map/sin | solution.py:215
  65.0 10.9 %all-to-all-done = bf16[16,24,640]{2,1,0:T(8,128)(2,1)S(1)} async-done(((bf16[16,24,640]{2,1,0:T(8,128)(2,1)}), bf16[16,24,640]{2,1,0:T(8,128)(2,1)S(1)}, u32[]{:S(2)}, u32[]{:S(2)}) %all-to-all-start) | async-done | bytes 491552 | tf_op jit(solution)/shard_map/all_to_all | solution.py:221
  75.9 0.1 copy.57
  76.0 0.3 reshape.194
  76.3 0.1 slice.36
  76.4 0.1 copy.53
  76.5 0.1 mul.90
  76.6 2.4 %fusion = (bf16[24,16,256]{2,1,0:T(8,128)(2,1)S(1)}, bf16[24,16,256]{2,1,0:T(8,128)(2,1)}) fusion(f32[24]{0:T(128)S(1)} %convert_multiply_fusion, f32[16,256]{1,0:T(8,128)S(1)} %mul.90), kind=kLoop, calls=%fused_computation.4 | loop fusion | flops 294912 | bytes 409696 | tf_op jit(solution)/shard_map/convert.1
  79.0 0.2 copy.54
  79.2 0.1 eq.52
  79.3 0.2 copy.50
  79.5 2.7 %reshape.188 = bf16[16,24,32,16]{1,0,3,2:T(8,128)(2,1)S(1)} reshape(bf16[384,512]{0,1:T(8,128)(2,1)S(1)} %copy.50) | data formatting | bytes 786432 | tf_op jit(solution)/shard_map/reshape | solution.py:236
  82.2 4.6 %copy.51 = bf16[24,32,16,16]{1,3,2,0:T(8,128)(2,1)} copy(bf16[24,32,16,16]{0,2,3,1:T(8,128)(2,1)S(1)} %bitcast.42) | data formatting | bytes 786432 | tf_op jit(solution)/shard_map/transpose | solution.py:237
  86.8 0.0 copy-start.3
  86.8 1.7 %copy.55.x_ref = bf16[24,32,256]{2,1,0:T(8,128)(2,1)S(1)} copy(bf16[24,32,256]{1,2,0:T(8,128)(2,1)} %bitcast.43) | data formatting | bytes 786432 | tf_op jit(solution)/shard_map/reshape | solution.py:237
  88.5 0.0 copy-done.3
  88.6 2.6 %shard_map.92 = f32[16,24,64]{2,1,0:T(8,128)S(1)} custom-call(bf16[24,32,256]{2,1,0:T(8,128)(2,1)S(1)} %copy.55.x_ref, bf16[24,32,256]{2,1,0:T(8,128)(2,1)S(1)} %pad_maximum_fusion.w_ref, f32[4,256]{1,0:T(4,128)S(1)} %fusion.16.mask_ref, f32[4,24,1024]{2,1,0:T(8,128)S(1)} %get-tuple-element.14.cos_ref, f32[4,24,1024]{2,1,0:T(8,128)S(1)} %get-tuple-element.13.sin_ref, ...), custom_call_target="tpu_custom_call" | custom-call | tf_op jit(solution)/shard_map/pallas_call | solution.py:239
  91.2 0.2 reshape.195
  91.3 11.3 %all_to_all.17 = f32[16,1,1536]{2,1,0:T(1,128)S(1)} all-to-all(f32[16,1,1536]{2,1,0:T(1,128)S(1)} %reshape.195), channel_id=1, replica_groups=mesh['grp'=2,'tile'=8,'stn'=2] {'tile','stn'}, dimensions={0} | all-to-all | bytes 196608 | tf_op jit(solution)/shard_map/all_to_all | solution.py:245
  102.7 0.5 broadcast.61
  103.2 0.9 reduce
  104.0 0.1 reshape.196
  104.1 0.8 copy.56
  (11 shorter events, 0.2 us)
Async XLA Ops:
  2.5 4.1 %copy-start.6 = (f32[16,16]{1,0:T(8,128)S(1)}, f32[16,16]{1,0:T(8,128)}, u32[]{:S(2)}) copy-start(f32[16,16]{1,0:T(8,128)} %param.13) | copy-start | bytes 3076
  2.5 4.2 %copy-start.5 = (f32[16,16]{1,0:T(8,128)S(1)}, f32[16,16]{1,0:T(8,128)}, u32[]{:S(2)}) copy-start(f32[16,16]{1,0:T(8,128)} %param.12) | copy-start | bytes 3076
  10.9 3.3 %copy-start = (bf16[16,2,126976]{2,1,0:T(2,128)(2,1)S(1)}, bf16[16,2,126976]{2,1,0:T(2,128)(2,1)}, u32[]{:S(2)}) copy-start(bf16[16,2,126976]{2,1,0:T(2,128)(2,1)} %param.9) | copy-start | bytes 24379396
  14.2 0.9 copy-start.2
  15.1 48.4 %copy-start.4 = (f32[1024,4]{0,1:T(4,128)S(1)}, f32[1024,4]{0,1:T(4,128)}, u32[]{:S(2)}) copy-start(f32[1024,4]{0,1:T(4,128)} %param.17) | copy-start | bytes 49156
  53.9 0.8 copy-start.1
  54.7 21.2 %all-to-all-start = ((bf16[16,24,640]{2,1,0:T(8,128)(2,1)}), bf16[16,24,640]{2,1,0:T(8,128)(2,1)S(1)}, u32[]{:S(2)}, u32[]{:S(2)}) async-start(bf16[16,24,640]{2,1,0:T(8,128)(2,1)} %bitcast.40), calls=%async_computation | async-start | bytes 983040 | tf_op jit(solution)/shard_map/all_to_all | solution.py:221
  86.8 1.7 %copy-start.3 = (bf16[24,16,256]{2,1,0:T(8,128)(2,1)S(1)}, bf16[24,16,256]{2,1,0:T(8,128)(2,1)}, u32[]{:S(2)}) copy-start(bf16[24,16,256]{2,1,0:T(8,128)(2,1)} %get-tuple-element.16) | copy-start | bytes 589828

commit v5 on v4

--- a/solution.py
+++ b/solution.py
@@ -15,7 +15,7 @@
 GROUP_AXES = ("tile", "stn")
 
 
-def filter_dft_kernel(frames, taps, x_ref, taps_ref, ca_ref, sa_ref, cb_ref, sb_ref, extra_ref, out_ref, filt, table, acc):
+def filter_dft_kernel(frames, taps, x_ref, taps_ref, ca_ref, sa_ref, cb_ref, sb_ref, extra_ref, out_ref, filt, mixed, table, acc):
     step = pl.program_id(0)
     antennas = x_ref.shape[0]
     selected = cb_ref.shape[0]
@@ -30,18 +30,23 @@
         table[0:selected, lanes] = (ca * cb - sa * sb).astype(jnp.bfloat16)
         table[selected : 2 * selected, lanes] = (sa * cb + ca * sb).astype(jnp.bfloat16)
         weights = [
-            jnp.broadcast_to(taps_ref[j : j + 1, lanes], (antennas, LANES)) for j in range(taps)
+            jnp.broadcast_to(taps_ref[j : j + 1, lanes], (2 * antennas, LANES))
+            for j in range(taps)
         ]
-        for r in range(2):
-            blocks = [
-                x_ref[:, k, r, lanes].astype(jnp.float32) for k in range(frames + taps - 1)
-            ]
-            for f in range(frames):
-                total = blocks[f] * weights[0]
-                for j in range(1, taps):
-                    total = total + blocks[f + j] * weights[j]
+        blocks = [
+            x_ref[:, k, :, lanes].reshape(2 * antennas, LANES).astype(jnp.float32)
+            for k in range(frames + taps - 1)
+        ]
+        for f in range(frames):
+            total = blocks[f] * weights[0]
+            for j in range(1, taps):
+                total = total + blocks[f + j] * weights[j]
+            mixed[f] = total
+            for r in range(2):
                 start = r * rows + f * antennas
-                filt[start : start + antennas, lanes] = total.astype(jnp.bfloat16)
+                filt[start : start + antennas, lanes] = mixed[
+                    f, pl.ds(r, antennas, stride=2), :
+                ].astype(jnp.bfloat16)
 
     product = lax.dot_general(
         table[...], filt[...], (((1,), (1,)), ((), ())), preferred_element_type=jnp.float32
@@ -105,6 +110,7 @@
         out_shape=jax.ShapeDtypeStruct((selected, width + extra.shape[1]), jnp.bfloat16),
         scratch_shapes=[
             pltpu.VMEM((width, CHUNK), jnp.bfloat16),
+            pltpu.VMEM((frames, 2 * antennas, LANES), jnp.float32),
             pltpu.VMEM((2 * selected, CHUNK), jnp.bfloat16),
             pltpu.VMEM((2 * selected, width), jnp.float32),
         ],

time: 106 us -> 117 us (1.10)
  Pallas kernels: 41.3 us -> 52.4 us
    pallas_call x1, Pallas kernels: 38.7 us -> 49.7 us  [channel_spectra(): pl.pallas_call(functools.partial(filter_dft_kernel, frames, taps), grid=(...]
  transfers between devices with their start and end apart: 1 -> 1, of which waited for: 1 -> 1; matrix products, arithmetic and copies ran while one was open for 3% -> 2% of each run, Pallas kernels for 0% -> 0%
where the time goes in v5:
time: 117 us; the launch traced here: 116 us
  Pallas kernels  52.4 us (45%)
  local copies, waits for them, and re-layouts  22.7 us (19%)
  blocking collectives  11.3 us (10%)
  other arithmetic  11 us (9%)
  waiting for transfers between devices  10.9 us (9%)
  starting transfers between devices  7.4 us (6%)
    pallas_call x1, Pallas kernels, channel_spectra(): pl.pallas_call(functools.partial(filter_dft_kernel, frames, taps), grid=(...  49.7 us
    all_to_all x1, blocking collectives, body(): lax.all_to_all(power, GROUP_AXES, split_axis=0, concat_axis=0, tiled=True)  11.3 us
    all_to_all x1, waiting for transfers between devices, body(): lax.all_to_all(spectra, GROUP_AXES, split_axis=0, concat_axis=0, tiled=True)  10.9 us
    unnamed x19, local copies, waits for them, and re-layouts  7.47 us
    all_to_all x1, starting transfers between devices, body(): lax.all_to_all(spectra, GROUP_AXES, split_axis=0, concat_axis=0, tiled=True)  7.4 us
    transpose x1, local copies, waits for them, and re-layouts, body(): spectra = spectra.transpose(1, 2, 0, 3).reshape(share, 2 * frames, total)  4.61 us
    reshape x1, local copies, waits for them, and re-layouts, body(): spectra = spectra[:, :width].reshape(devices, share, 2 * frames, antennas)  2.73 us
    pallas_call x1, Pallas kernels, body(): pl.pallas_call(functools.partial(beam_power_kernel, frames, 1.0 / (frames...  2.61 us
  transfers between devices with their start and end apart: 1, of which 1 were waited for; matrix products, arithmetic and copies ran while one was open for 2% of the time, Pallas kernels for 0%

profile of v5, /device:TPU:0, one launch (start us, length us, event | category | flops | bytes accessed | tf_op | source)
XLA Modules:
  0.0 115.9 jit_solution(18012794620275231226)
XLA Ops:
  0.0 1.5 %fusion.9 = (f32[384,128]{1,0:T(8,128)S(1)}, f32[384,128]{1,0:T(8,128)S(1)}) fusion(s32[384]{0:T(512)} %param.11), kind=kLoop, calls=%fused_computation.20 | loop fusion | flops 688128 | bytes 394752 | tf_op jit(solution)/shard_map/sin | solution.py:77
  1.5 1.0 sine_multiply_fusion
  2.5 0.0 copy-start.6
  2.5 0.0 copy-start.5
  2.5 0.5 copy.45
  3.0 0.6 reshape.187
  3.7 1.3 %copy.46 = f32[384,8,4]{2,0,1:T(8,128)S(1)} copy(f32[384,8,4]{0,2,1:T(4,128)} %reshape.187) | data formatting | bytes 98304 | tf_op jit(solution)/shard_map/reshape | solution.py:95
  5.0 0.7 iota_compare_fusion.1
  5.7 0.9 select_reduce_fusion.1
  6.6 0.0 copy-done.6
  6.6 0.1 select_reduce_fusion
  6.7 0.0 copy-done.5
  6.7 0.6 pad_maximum_fusion.1
  7.4 1.4 %copy.58 = bf16[17,3,16]{0,2,1:T(8,128)(2,1)} copy(bf16[17,3,16]{2,0,1:T(8,128)(2,1)} %pad_maximum_fusion.1) | data formatting | bytes 3264
  8.8 0.7 pad.8.clone
  9.5 0.7 copy.59
  10.2 0.7 pad.9.clone
  10.9 0.0 copy-start
  10.9 3.3 %copy-done = bf16[16,2,126976]{2,1,0:T(2,128)(2,1)S(1)} copy-done((bf16[16,2,126976]{2,1,0:T(2,128)(2,1)S(1)}, bf16[16,2,126976]{2,1,0:T(2,128)(2,1)}, u32[]{:S(2)}) %copy-start) | copy-done | bytes 8126488
  14.2 0.0 copy-start.2
  14.2 0.9 copy-done.2
  15.1 0.0 copy-start.4
  15.1 49.7 %shard_map.91 = bf16[384,640]{1,0:T(8,128)(2,1)S(1)} custom-call(bf16[16,31,2,4096]{3,2,1,0:T(2,128)(2,1)S(1)} %bitcast.37, f32[16,4096]{1,0:T(8,128)S(1)} %copy-done.2, f32[8,384,4]{2,1,0:T(8,128)S(1)} %bitcast.38, f32[8,384,4]{2,1,0:T(8,128)S(1)} %bitcast.39, f32[384,128]{1,0:T(8,128)S(1)} %get-tuple-element.11.cb_ref, ...), custom_call_target="tpu_custom_call" | custom-call | tf_op jit(solution)/shard_map/pallas_call | solution.py:97
  64.9 0.0 copy-start.1
  64.9 0.8 copy-done.1
  65.7 7.4 %all-to-all-start = ((bf16[16,24,640]{2,1,0:T(8,128)(2,1)}), bf16[16,24,640]{2,1,0:T(8,128)(2,1)S(1)}, u32[]{:S(2)}, u32[]{:S(2)}) async-start(bf16[16,24,640]{2,1,0:T(8,128)(2,1)} %bitcast.40), calls=%async_computation | async-start | bytes 983040 | tf_op jit(solution)/shard_map/all_to_all | solution.py:227
  73.1 0.8 convert_multiply_fusion
  73.9 0.7 fusion.11.onehot_ref
  74.5 0.0 copy-done.4
  74.6 1.4 %multiply_sine_fusion = (f32[4,24,1024]{2,1,0:T(8,128)S(1)}, f32[4,24,1024]{2,1,0:T(8,128)S(1)}) fusion(f32[24]{0:T(128)S(1)} %convert_multiply_fusion, f32[4,1024]{1,0:T(4,128)S(1)} %bitcast.49), kind=kLoop, calls=%fused_computation | loop fusion | flops 98304 | bytes 802912 | tf_op jit(solution)/shard_map/sin | solution.py:221
  76.0 10.9 %all-to-all-done = bf16[16,24,640]{2,1,0:T(8,128)(2,1)S(1)} async-done(((bf16[16,24,640]{2,1,0:T(8,128)(2,1)}), bf16[16,24,640]{2,1,0:T(8,128)(2,1)S(1)}, u32[]{:S(2)}, u32[]{:S(2)}) %all-to-all-start) | async-done | bytes 491552 | tf_op jit(solution)/shard_map/all_to_all | solution.py:227
  86.9 0.1 copy.57
  87.0 0.3 reshape.194
  87.3 0.1 slice.36
  87.4 0.1 copy.53
  87.5 0.1 mul.90
  87.6 2.4 %fusion = (bf16[24,16,256]{2,1,0:T(8,128)(2,1)S(1)}, bf16[24,16,256]{2,1,0:T(8,128)(2,1)}) fusion(f32[24]{0:T(128)S(1)} %convert_multiply_fusion, f32[16,256]{1,0:T(8,128)S(1)} %mul.90), kind=kLoop, calls=%fused_computation.4 | loop fusion | flops 294912 | bytes 409696 | tf_op jit(solution)/shard_map/convert.1
  90.0 0.2 copy.54
  90.2 0.1 eq.52
  90.3 0.2 copy.50
  90.5 2.7 %reshape.188 = bf16[16,24,32,16]{1,0,3,2:T(8,128)(2,1)S(1)} reshape(bf16[384,512]{0,1:T(8,128)(2,1)S(1)} %copy.50) | data formatting | bytes 786432 | tf_op jit(solution)/shard_map/reshape | solution.py:242
  93.2 4.6 %copy.51 = bf16[24,32,16,16]{1,3,2,0:T(8,128)(2,1)} copy(bf16[24,32,16,16]{0,2,3,1:T(8,128)(2,1)S(1)} %bitcast.42) | data formatting | bytes 786432 | tf_op jit(solution)/shard_map/transpose | solution.py:243
  97.8 0.0 copy-start.3
  97.8 1.7 %copy.55.x_ref = bf16[24,32,256]{2,1,0:T(8,128)(2,1)S(1)} copy(bf16[24,32,256]{1,2,0:T(8,128)(2,1)} %bitcast.43) | data formatting | bytes 786432 | tf_op jit(solution)/shard_map/reshape | solution.py:243
  99.5 0.0 copy-done.3
  99.6 2.6 %shard_map.92 = f32[16,24,64]{2,1,0:T(8,128)S(1)} custom-call(bf16[24,32,256]{2,1,0:T(8,128)(2,1)S(1)} %copy.55.x_ref, bf16[24,32,256]{2,1,0:T(8,128)(2,1)S(1)} %pad_maximum_fusion.w_ref, f32[4,256]{1,0:T(4,128)S(1)} %fusion.16.mask_ref, f32[4,24,1024]{2,1,0:T(8,128)S(1)} %get-tuple-element.14.cos_ref, f32[4,24,1024]{2,1,0:T(8,128)S(1)} %get-tuple-element.13.sin_ref, ...), custom_call_target="tpu_custom_call" | custom-call | tf_op jit(solution)/shard_map/pallas_call | solution.py:245
  102.2 0.2 reshape.195
  102.4 11.3 %all_to_all.17 = f32[16,1,1536]{2,1,0:T(1,128)S(1)} all-to-all(f32[16,1,1536]{2,1,0:T(1,128)S(1)} %reshape.195), channel_id=1, replica_groups=mesh['grp'=2,'tile'=8,'stn'=2] {'tile','stn'}, dimensions={0} | all-to-all | bytes 196608 | tf_op jit(solution)/shard_map/all_to_all | solution.py:251
  113.6 0.5 broadcast.61
  114.2 0.9 reduce
  115.0 0.1 reshape.196
  115.1 0.8 copy.56
  (11 shorter events, 0.2 us)
Async XLA Ops:
  2.5 4.1 %copy-start.6 = (f32[16,16]{1,0:T(8,128)S(1)}, f32[16,16]{1,0:T(8,128)}, u32[]{:S(2)}) copy-start(f32[16,16]{1,0:T(8,128)} %param.13) | copy-start | bytes 3076
  2.5 4.2 %copy-start.5 = (f32[16,16]{1,0:T(8,128)S(1)}, f32[16,16]{1,0:T(8,128)}, u32[]{:S(2)}) copy-start(f32[16,16]{1,0:T(8,128)} %param.12) | copy-start | bytes 3076
  10.9 3.3 %copy-start = (bf16[16,2,126976]{2,1,0:T(2,128)(2,1)S(1)}, bf16[16,2,126976]{2,1,0:T(2,128)(2,1)}, u32[]{:S(2)}) copy-start(bf16[16,2,126976]{2,1,0:T(2,128)(2,1)} %param.9) | copy-start | bytes 24379396
  14.2 0.9 copy-start.2
  15.1 59.4 %copy-start.4 = (f32[1024,4]{0,1:T(4,128)S(1)}, f32[1024,4]{0,1:T(4,128)}, u32[]{:S(2)}) copy-start(f32[1024,4]{0,1:T(4,128)} %param.17) | copy-start | bytes 49156
  64.9 0.8 copy-start.1
  65.7 21.2 %all-to-all-start = ((bf16[16,24,640]{2,1,0:T(8,128)(2,1)}), bf16[16,24,640]{2,1,0:T(8,128)(2,1)S(1)}, u32[]{:S(2)}, u32[]{:S(2)}) async-start(bf16[16,24,640]{2,1,0:T(8,128)(2,1)} %bitcast.40), calls=%async_computation | async-start | bytes 983040 | tf_op jit(solution)/shard_map/all_to_all | solution.py:227
  97.8 1.7 %copy-start.3 = (bf16[24,16,256]{2,1,0:T(8,128)(2,1)S(1)}, bf16[24,16,256]{2,1,0:T(8,128)(2,1)}, u32[]{:S(2)}) copy-start(bf16[24,16,256]{2,1,0:T(8,128)(2,1)} %get-tuple-element.16) | copy-start | bytes 589828

commit v6 on v4

--- a/solution.py
+++ b/solution.py
@@ -108,7 +108,7 @@
             pltpu.VMEM((2 * selected, CHUNK), jnp.bfloat16),
             pltpu.VMEM((2 * selected, width), jnp.float32),
         ],
-        compiler_params=pltpu.CompilerParams(vmem_limit_bytes=32 * 1024 * 1024),
+        compiler_params=pltpu.CompilerParams(vmem_limit_bytes=60 * 1024 * 1024),
     )(x, filter_taps, ca, sa, cb, sb, extra)
 
 

time: 106 us -> 97.6 us (0.921)
  local copies, waits for them, and re-layouts: 22.7 us -> 16 us
  other arithmetic: 11 us -> 9.15 us
    unnamed x19, local copies, waits for them, and re-layouts: 7.47 us -> 0.57 us
    reshape x2, local copies, waits for them, and re-layouts: 0.51 us -> 1.68 us  [channel_spectra(): ca = ca.reshape(selected, steps, pieces).transpose(1, 0, 2)]
  transfers between devices with their start and end apart: 1 -> 1, of which waited for: 1 -> 1; matrix products, arithmetic and copies ran while one was open for 3% -> 2% of each run, Pallas kernels for 0% -> 0%
where the time goes in v6:
time: 97.6 us; the launch traced here: 97.2 us
  Pallas kernels  41.6 us (43%)
  local copies, waits for them, and re-layouts  16 us (16%)
  waiting for transfers between devices  11.5 us (12%)
  blocking collectives  11.3 us (12%)
  other arithmetic  9.15 us (9%)
  starting transfers between devices  7.39 us (8%)
    pallas_call x1, Pallas kernels, channel_spectra(): pl.pallas_call(functools.partial(filter_dft_kernel, frames, taps), grid=(...  39 us
    all_to_all x1, waiting for transfers between devices, body(): lax.all_to_all(spectra, GROUP_AXES, split_axis=0, concat_axis=0, tiled=True)  11.5 us
    all_to_all x1, blocking collectives, body(): lax.all_to_all(power, GROUP_AXES, split_axis=0, concat_axis=0, tiled=True)  11.3 us
    all_to_all x1, starting transfers between devices, body(): lax.all_to_all(spectra, GROUP_AXES, split_axis=0, concat_axis=0, tiled=True)  7.39 us
    transpose x1, local copies, waits for them, and re-layouts, body(): spectra = spectra.transpose(1, 2, 0, 3).reshape(share, 2 * frames, total)  4.61 us
    reshape x1, local copies, waits for them, and re-layouts, body(): spectra = spectra[:, :width].reshape(devices, share, 2 * frames, antennas)  2.73 us
    pallas_call x1, Pallas kernels, body(): pl.pallas_call(functools.partial(beam_power_kernel, frames, 1.0 / (frames...  2.6 us
    another operation x2, other arithmetic  2.38 us
  transfers between devices with their start and end apart: 1, of which 1 were waited for; matrix products, arithmetic and copies ran while one was open for 2% of the time, Pallas kernels for 0%

profile of v6, /device:TPU:0, one launch (start us, length us, event | category | flops | bytes accessed | tf_op | source)
XLA Modules:
  0.0 97.2 jit_solution(15999310357470091189)
XLA Ops:
  0.0 2.3 %fusion.9 = (f32[384,128]{1,0:T(8,128)}, f32[384,128]{1,0:T(8,128)}) fusion(s32[384]{0:T(512)} %param.11), kind=kLoop, calls=%fused_computation.20 | loop fusion | flops 688128 | bytes 394752 | tf_op jit(solution)/shard_map/sin | solution.py:72
  2.3 1.0 sine_multiply_fusion
  3.3 0.0 copy-start.5
  3.3 0.0 copy-start.6
  3.3 0.0 copy-start.3
  3.3 0.0 copy-start.2
  3.3 1.7 %copy.45 = f32[384,8,4]{2,0,1:T(8,128)} copy(f32[384,8,4]{0,2,1:T(4,128)S(1)} %reshape.186) | data formatting | bytes 98304 | tf_op jit(solution)/shard_map/reshape | solution.py:89
  5.0 1.7 %copy.46 = f32[384,8,4]{2,0,1:T(8,128)} copy(f32[384,8,4]{0,2,1:T(4,128)S(1)} %reshape.187) | data formatting | bytes 98304 | tf_op jit(solution)/shard_map/reshape | solution.py:90
  6.7 0.0 copy-done.5
  6.7 0.1 iota_compare_fusion.1
  6.7 0.0 copy-done.6
  6.7 0.2 select_reduce_fusion.1
  6.9 0.0 copy-done.3
  6.9 0.1 select_reduce_fusion
  7.0 0.0 copy-done.2
  7.1 0.1 copy.58
  7.2 0.1 copy.59
  7.3 0.7 tile.4
  8.0 0.0 copy-start.4
  8.0 0.0 copy-start.1
  8.0 39.0 %shard_map.91 = bf16[384,640]{1,0:T(8,128)(2,1)} custom-call(bf16[16,31,2,4096]{3,2,1,0:T(2,128)(2,1)} %bitcast.38, f32[16,4096]{1,0:T(8,128)} %taps_ref.1, f32[8,384,4]{2,1,0:T(8,128)} %bitcast.39, f32[8,384,4]{2,1,0:T(8,128)} %bitcast.40, f32[384,128]{1,0:T(8,128)} %get-tuple-element.11.cb_ref, f32[384,128]{1,0:T(8,128)} %get-tuple-element.12.sb_ref, ...), custom_call_target="tpu_custom_call" | custom-call | tf_op jit(solution)/shard_map/pallas_call | solution.py:92
  47.0 7.4 %all-to-all-start = ((bf16[16,24,640]{2,1,0:T(8,128)(2,1)}), bf16[16,24,640]{2,1,0:T(8,128)(2,1)S(1)}, u32[]{:S(2)}, u32[]{:S(2)}) async-start(bf16[16,24,640]{2,1,0:T(8,128)(2,1)} %bitcast.44), calls=%async_computation | async-start | bytes 983040 | tf_op jit(solution)/shard_map/all_to_all | solution.py:221
  54.4 0.8 convert_multiply_fusion
  55.2 0.0 copy-done.4
  55.2 0.0 copy-done.1
  55.2 1.4 %multiply_sine_fusion = (f32[4,24,1024]{2,1,0:T(8,128)S(1)}, f32[4,24,1024]{2,1,0:T(8,128)S(1)}) fusion(f32[24]{0:T(128)S(1)} %convert_multiply_fusion, f32[4,1024]{1,0:T(4,128)S(1)} %bitcast.49), kind=kLoop, calls=%fused_computation | loop fusion | flops 98304 | bytes 802912 | tf_op jit(solution)/shard_map/sin | solution.py:215
  56.6 11.5 %all-to-all-done = bf16[16,24,640]{2,1,0:T(8,128)(2,1)S(1)} async-done(((bf16[16,24,640]{2,1,0:T(8,128)(2,1)}), bf16[16,24,640]{2,1,0:T(8,128)(2,1)S(1)}, u32[]{:S(2)}, u32[]{:S(2)}) %all-to-all-start) | async-done | bytes 491552 | tf_op jit(solution)/shard_map/all_to_all | solution.py:221
  68.2 0.1 copy.57
  68.3 0.3 reshape.194
  68.6 0.1 slice.36
  68.7 0.1 copy.53
  68.8 0.1 mul.90
  68.9 2.4 %fusion = (bf16[24,16,256]{2,1,0:T(8,128)(2,1)S(1)}, bf16[24,16,256]{2,1,0:T(8,128)(2,1)}) fusion(f32[24]{0:T(128)S(1)} %convert_multiply_fusion, f32[16,256]{1,0:T(8,128)S(1)} %mul.90), kind=kLoop, calls=%fused_computation.4 | loop fusion | flops 294912 | bytes 409696 | tf_op jit(solution)/shard_map/convert.1
  71.3 0.2 copy.54
  71.5 0.1 eq.52
  71.6 0.2 copy.50
  71.8 2.7 %reshape.188 = bf16[16,24,32,16]{1,0,3,2:T(8,128)(2,1)S(1)} reshape(bf16[384,512]{0,1:T(8,128)(2,1)S(1)} %copy.50) | data formatting | bytes 786432 | tf_op jit(solution)/shard_map/reshape | solution.py:236
  74.5 4.6 %copy.51 = bf16[24,32,16,16]{1,3,2,0:T(8,128)(2,1)} copy(bf16[24,32,16,16]{0,2,3,1:T(8,128)(2,1)S(1)} %bitcast.37) | data formatting | bytes 786432 | tf_op jit(solution)/shard_map/transpose | solution.py:237
  79.1 0.0 copy-start
  79.1 1.7 %copy.55.x_ref = bf16[24,32,256]{2,1,0:T(8,128)(2,1)S(1)} copy(bf16[24,32,256]{1,2,0:T(8,128)(2,1)} %bitcast.41) | data formatting | bytes 786432 | tf_op jit(solution)/shard_map/reshape | solution.py:237
  80.8 0.0 copy-done
  80.9 2.6 %shard_map.92 = f32[16,24,64]{2,1,0:T(8,128)S(1)} custom-call(bf16[24,32,256]{2,1,0:T(8,128)(2,1)S(1)} %copy.55.x_ref, bf16[24,32,256]{2,1,0:T(8,128)(2,1)S(1)} %pad_maximum_fusion.w_ref, f32[4,256]{1,0:T(4,128)S(1)} %fusion.16.mask_ref, f32[4,24,1024]{2,1,0:T(8,128)S(1)} %get-tuple-element.14.cos_ref, f32[4,24,1024]{2,1,0:T(8,128)S(1)} %get-tuple-element.13.sin_ref, ...), custom_call_target="tpu_custom_call" | custom-call | tf_op jit(solution)/shard_map/pallas_call | solution.py:239
  83.5 0.2 reshape.195
  83.7 11.3 %all_to_all.17 = f32[16,1,1536]{2,1,0:T(1,128)S(1)} all-to-all(f32[16,1,1536]{2,1,0:T(1,128)S(1)} %reshape.195), channel_id=1, replica_groups=mesh['grp'=2,'tile'=8,'stn'=2] {'tile','stn'}, dimensions={0} | all-to-all | bytes 196608 | tf_op jit(solution)/shard_map/all_to_all | solution.py:245
  95.0 0.5 broadcast.61
  95.5 0.9 reduce
  96.4 0.1 reshape.196
  96.5 0.8 copy.56
  (15 shorter events, 0.2 us)
Async XLA Ops:
  3.3 3.4 %copy-start.5 = (s32[16]{0:T(128)S(1)}, s32[16]{0:T(128)}, u32[]{:S(2)}) copy-start(s32[16]{0:T(128)} %param.14) | copy-start | bytes 196
  3.3 3.5 %copy-start.6 = (s32[16]{0:T(128)S(1)}, s32[16]{0:T(128)}, u32[]{:S(2)}) copy-start(s32[16]{0:T(128)} %param.15) | copy-start | bytes 196
  3.3 3.6 %copy-start.3 = (f32[16,16]{1,0:T(8,128)S(1)}, f32[16,16]{1,0:T(8,128)}, u32[]{:S(2)}) copy-start(f32[16,16]{1,0:T(8,128)} %param.13) | copy-start | bytes 3076
  3.3 3.7 %copy-start.2 = (f32[16,16]{1,0:T(8,128)S(1)}, f32[16,16]{1,0:T(8,128)}, u32[]{:S(2)}) copy-start(f32[16,16]{1,0:T(8,128)} %param.12) | copy-start | bytes 3076
  8.0 47.2 %copy-start.4 = (s32[1024]{0:T(1024)S(1)}, s32[1024]{0:T(1024)}, u32[]{:S(2)}) copy-start(s32[1024]{0:T(1024)} %param.16) | copy-start | bytes 12292
  8.0 47.2 %copy-start.1 = (f32[1024,4]{0,1:T(4,128)S(1)}, f32[1024,4]{0,1:T(4,128)}, u32[]{:S(2)}) copy-start(f32[1024,4]{0,1:T(4,128)} %param.17) | copy-start | bytes 49156
  47.0 21.2 %all-to-all-start = ((bf16[16,24,640]{2,1,0:T(8,128)(2,1)}), bf16[16,24,640]{2,1,0:T(8,128)(2,1)S(1)}, u32[]{:S(2)}, u32[]{:S(2)}) async-start(bf16[16,24,640]{2,1,0:T(8,128)(2,1)} %bitcast.44), calls=%async_computation | async-start | bytes 983040 | tf_op jit(solution)/shard_map/all_to_all | solution.py:221
  79.1 1.7 %copy-start = (bf16[24,16,256]{2,1,0:T(8,128)(2,1)S(1)}, bf16[24,16,256]{2,1,0:T(8,128)(2,1)}, u32[]{:S(2)}) copy-start(bf16[24,16,256]{2,1,0:T(8,128)(2,1)} %get-tuple-element.16) | copy-start | bytes 589828
